TPU v7x, 128 devices: a whole 4x4x4 slice. The times are simulated.
128 devices in a mesh: slab: 16 (over x_hi, y, core), cross: 8 (over x_lo, z).
Axes of the slice: x: 4 (x_hi: 2, x_lo: 2; x = x_hi * 2 + x_lo), y: 4, z: 4, core: 2. Of those that a mesh axis runs over, the one named last changes fastest.
Arguments:
- velocity: float32 [3, 256, 256, 256], P(None, 'slab', 'cross'), may hold values from -6 to 6
- pressure: float32 [256, 256, 256], P('slab', 'cross'), may hold values from -6 to 6
- inv_influence: bfloat16 [16384, 16384], P('cross', 'slab'), may hold values from -0.046875 to 0.046875
- normals: float32 [3, 16384], P(None, 'slab'), may hold values from -3 to 3
- sample_cells: int32 [16384, 256], P('slab'), may hold values from 0 to 65535
- tangents: float32 [3, 8, 16, 128], P(None, 'cross', 'slab'), may hold values from -5 to 5
- force_owner: int32 [16384], replicated, may hold values from 0 to 15
- force_cell: int32 [16384], replicated, may hold values from 0 to 8191
Outputs:
- velocity_new: float32 [3, 256, 256, 256], P(None, 'slab', 'cross')
- pressure_new: float32 [256, 256, 256], P('slab', 'cross')
Inputs may be any that keep to these rules, and one draw needn't show every extreme that they name: `force_owner`: A few owners take most panels.
All inputs are finite; a program needn't handle non-finite values.
Results may differ from a plain program's by a relative error of at most 0.0003.
Values sent between devices are 32-bit elements; how exact they have to be, the bound alone decides.
A program may use at most 384 MiB of HBM per device.

v0:
```python
import jax
import jax.numpy as jnp
from jax import lax
from jax.sharding import PartitionSpec as P

time_step = 0.5
viscosity = 0.1


def padded_2(block, sides, width):
    for axis, dim in sides:
        count = lax.axis_size(axis)
        forward = [(i, i + 1) for i in range(count - 1)]
        backward = [(target, source) for source, target in forward]
        low = lax.ppermute(
            lax.slice_in_dim(block, block.shape[dim] - width, None, axis=dim), axis, forward
        )
        high = lax.ppermute(lax.slice_in_dim(block, 0, width, axis=dim), axis, backward)
        block = jnp.concatenate([low, block, high], axis=dim)
    return block


def broadcast(value, axis, source):
    kept = jnp.where(lax.axis_index(axis) == source, value, 0).astype(value.dtype)
    return lax.psum(kept, axis)


def around_sum(padded):
    total = padded[:, 2:, 1:-1, 1:-1] + padded[:, :-2, 1:-1, 1:-1]
    total = total + padded[:, 1:-1, 2:, 1:-1] + padded[:, 1:-1, :-2, 1:-1]
    return total + padded[:, 1:-1, 1:-1, 2:] + padded[:, 1:-1, 1:-1, :-2]


def slopes(padded, first, second, third):
    slope_x = padded[first, 2:, 1:-1, 1:-1] - padded[first, :-2, 1:-1, 1:-1]
    slope_y = padded[second, 1:-1, 2:, 1:-1] - padded[second, 1:-1, :-2, 1:-1]
    slope_z = padded[third, 1:-1, 1:-1, 2:] - padded[third, 1:-1, 1:-1, :-2]
    return (slope_x, slope_y, slope_z)


def extend(field, width):
    return padded_2(field, (("slab", 1), ("cross", 2)), width)


def pad_depth(field):
    return jnp.pad(field, ((0, 0), (0, 0), (0, 0), (1, 1)))


def body(
    velocity, pressure, inv_influence, normals, sample_cells, tangents, force_owner, force_cell
):
    slab_count = lax.axis_size("slab")
    cross_count = lax.axis_size("cross")
    slab_index = lax.axis_index("slab")
    cross_index = lax.axis_index("cross")
    root_slab = slab_count // 2 - 1
    cells_x, cells_y, cells_z = pressure.shape
    own_slice = velocity[:, cells_x // 2]
    full_plane = lax.all_gather(own_slice, "cross", axis=1, tiled=True)
    inflow = broadcast(full_plane, "slab", root_slab)
    flat_inflow = inflow.reshape(3, -1)
    sampled = flat_inflow[:, sample_cells]
    normal_flow = (
        normals[0][:, None] * sampled[0]
        + normals[1][:, None] * sampled[1]
        + normals[2][:, None] * sampled[2]
    ).astype(jnp.bfloat16)
    panel_rows = tangents.shape[3]
    strength = lax.psum_scatter(
        jnp.dot(inv_influence, normal_flow, preferred_element_type=jnp.float32),
        "slab",
        scatter_dimension=0,
        tiled=True,
    )
    loading = jnp.mean(strength * strength, axis=1)
    forces = tangents.reshape(3, panel_rows) * loading[None, :]
    gathered = lax.all_gather(forces, ("slab", "cross"), axis=1, tiled=True)
    all_forces = (
        gathered.reshape(3, slab_count, cross_count, panel_rows)
        .transpose(0, 2, 1, 3)
        .reshape(3, -1)
    )
    upstream = slab_index - root_slab
    owner_id = cross_index + cross_count * upstream
    holds = (upstream >= 0) & (upstream <= 1)
    pushed = jnp.where(((force_owner == owner_id) & holds)[None, :], all_forces, 0.0)
    plane_force = jnp.zeros((3, cells_y * cells_z), jnp.float32).at[:, force_cell].add(pushed)
    plane_x = jnp.where(upstream == 0, cells_x - 1, 0)
    selector = (jnp.arange(cells_x) == plane_x).astype(jnp.float32)
    body_force = plane_force.reshape(3, 1, cells_y, cells_z) * selector[None, :, None, None]
    beside_all = around_sum(pad_depth(extend(velocity, 1)))
    predicted = velocity + time_step * (viscosity * (beside_all - 6.0 * velocity) + body_force)
    slope_x, slope_y, slope_z = slopes(pad_depth(extend(predicted, 1)), 0, 1, 2)
    divergence = 0.5 * (slope_x + slope_y + slope_z)
    correction = pressure
    for repeat in range(2):
        around_field = around_sum(pad_depth(extend(correction[None], 1)))[0]
        correction = (around_field - divergence) / 6.0
    grad_x, grad_y, grad_z = slopes(pad_depth(extend(correction[None], 1)), 0, 0, 0)
    velocity_new = predicted - 0.5 * jnp.stack([grad_x, grad_y, grad_z])
    return (velocity_new, correction)


def solution(mesh):
    return jax.shard_map(
        body,
        mesh=mesh,
        in_specs=(
            P(None, "slab", "cross", None),
            P("slab", "cross", None),
            P("cross", "slab"),
            P(None, "slab"),
            P("slab", None),
            P(None, "cross", "slab", None),
            P(),
            P(),
        ),
        out_specs=(P(None, "slab", "cross", None), P("slab", "cross", None)),
        check_vma=False,
    )
```

profile of v0, /device:TPU:6, one launch (start us, length us, event | category | flops | bytes accessed | tf_op | source)
XLA Modules:
  0.0 1917.0 jit_solution(3689134225254673183)
XLA Ops:
  8.2 30.3 %all-gather = f32[3,1,256,256]{3,2,1,0:T(8,128)S(1)} all-gather(f32[3,1,32,256]{3,2,1,0:T(8,128)S(1)} %get-tuple-element.10), channel_id=2, replica_groups=mesh['slab'=16,'cross'=8] {'cross'}, dimensions={2}, use_global_device_ids=true | all-gather | bytes 884736 | tf_op jit(solution)/shard_map/all_gather | solution.py:59
  38.6 16.8 copy.15
  58.0 373.5 %all-reduce.7.cloned.1.call-done = f32[3,65536]{0,1:T(8,128)} async-done(((f32[3,65536]{0,1:T(8,128)}), f32[3,65536]{0,1:T(8,128)}) %all-reduce.7.cloned.1.call-update) | async-done | bytes 786448 | tf_op jit(solution)/shard_map/psum | solution.py:25
  431.5 876.4 %gather_fusion = f32[262144,3]{1,0:T(8,128)} fusion(f32[3,65536]{0,1:T(8,128)} %all-reduce.7.cloned.1.call-done, s32[262144]{0:T(1024)S(1)} %broadcast_clamp_fusion), kind=kCustom, calls=%fused_computation | custom fusion | bytes 7340032 | tf_op jit(solution)/shard_map/gather | solution.py:62
  1307.9 69.6 %copy.16 = f32[1024,256,3]{1,0,2:T(8,128)S(1)} copy(f32[1024,256,3]{2,1,0:T(8,128)} %bitcast.2) | data formatting | bytes 6291456 | tf_op jit(solution)/shard_map/gather | solution.py:62
  1377.5 5.3 convolution_bitcast_fusion
  1384.9 7.3 collective-permute-start
  1400.0 4.5 collective-permute-start.2
  1406.4 6.2 collective-permute-done.3
  1414.1 39.3 %reduce-scatter.2.cloned.1.call-done = f32[128,256]{0,1:T(8,128)} async-done(((f32[2048,256]{0,1:T(8,128)}), f32[128,256]{0,1:T(8,128)}) %reduce-scatter.2.cloned.1.call-update) | async-done | bytes 131088 | tf_op jit(solution)/shard_map/reduce_scatter | solution.py:69
  1454.3 268.7 %all_gather.7 = f32[3,16384]{1,0:T(4,128)S(1)} all-gather(f32[3,128]{1,0:T(4,128)S(1)} %bitcast_multiply_fusion), channel_id=1, replica_groups=mesh['slab'=16,'cross'=8] {'slab','cross'}, dimensions={1}, use_global_device_ids=true | all-gather | bytes 198144 | tf_op jit(solution)/shard_map/all_gather | solution.py:77
  1723.1 4.7 copy.17
  1727.7 12.6 bitcast_select_fusion
  1740.3 81.9 %scatter_custom_fusion = f32[3,8192]{0,1:T(8,128)} fusion(s32[16384]{0:T(1024)} %compare_select_fusion.1, f32[3,16384]{0,1:T(8,128)} %bitcast_select_fusion, f32[]{:T(128)} %constant.17.clone.1), kind=kCustom, calls=%fused_computation.2 | custom fusion | flops 49152 | bytes 8487424 | tf_op jit(solution)/shard_map/scatter-add | solution.py:87
  1825.8 5.1 fusion.8
  1836.0 5.6 collective-permute-start.6
  1843.7 6.0 collective-permute-start.10
  1852.9 4.9 collective-permute-done.11
  1862.4 5.4 collective-permute-start.12
  1869.8 6.9 collective-permute-done.13
  1878.6 3.9 collective-permute-start.15
  1882.6 3.8 collective-permute-done.15
  1891.7 6.4 collective-permute-done.17
  1900.1 3.9 collective-permute-start.19
  (97 shorter events, 53.3 us)
Async XLA Ops:
  7.2 424.3 %all-reduce.7.cloned.1.call-start = ((), (), s32[]{:S(2)}) async-start(), calls=%async_computation.1 | async-start | bytes 67108864 | tf_op jit(solution)/shard_map/psum | solution.py:25
  55.4 1397.9 %reduce-scatter.2.cloned.1.call-start = ((), (), s32[]{:S(2)}) async-start(), calls=%async_computation.2 | async-start | bytes 2228224 | tf_op jit(solution)/shard_map/reduce_scatter | solution.py:69
  1382.9 16.3 collective-permute-start.1
  1384.9 14.9 collective-permute-start
  1393.6 441.6 %collective-permute-start.4 = (f32[1,1,32,256]{3,2,1,0:T(8,128)}, f32[1,1,32,256]{3,2,1,0:T(8,128)S(1)}, u32[]{:S(2)}, u32[]{:S(2)}) collective-permute-start(f32[1,1,32,256]{3,2,1,0:T(8,128)} %get-tuple-element.26), channel_id=1, source_target_pairs={{8,0},{16,8},{24,16},{32,24},{40,32},{48,40},{56,48},{64,56},{72,6... | collective-permute-start | bytes 98312 | tf_op jit(solution)/shard_map/ppermute | solution.py:18
  1395.5 439.7 %collective-permute-start.5 = (f32[1,1,32,256]{3,2,1,0:T(8,128)}, f32[1,1,32,256]{3,2,1,0:T(8,128)}, u32[]{:S(2)}, u32[]{:S(2)}) collective-permute-start(f32[1,1,32,256]{3,2,1,0:T(8,128)} %get-tuple-element.25), channel_id=1, source_target_pairs={{0,8},{8,16},{16,24},{24,32},{32,40},{40,48},{48,56},{56,64},{64,7... | collective-permute-start | bytes 98312 | tf_op jit(solution)/shard_map/ppermute | solution.py:15
  1400.0 6.4 collective-permute-start.2
  1404.4 8.2 collective-permute-start.3
  1406.4 47.9 %copy-start.14 = (f32[3,1,1,128]{3,2,1,0:T(1,128)S(1)}, f32[3,1,1,128]{3,2,1,0:T(1,128)}, u32[]{:S(2)}) copy-start(f32[3,1,1,128]{3,2,1,0:T(1,128)} %param.13) | copy-start | bytes 4612
  1830.9 12.7 collective-permute-start.8
  1832.8 10.8 collective-permute-start.9
  1836.0 15.6 collective-permute-start.6
  1841.6 10.0 collective-permute-start.7
  1843.7 9.3 collective-permute-start.10
  1849.7 8.2 collective-permute-start.11
  1862.4 7.3 collective-permute-start.12
  1867.8 8.8 collective-permute-start.13
  1876.7 5.9 collective-permute-start.14
  1878.6 7.8 collective-permute-start.15
  1887.3 21.4 %copy-start = (f32[1,16,32,256]{3,2,1,0:T(8,128)}, f32[1,16,32,256]{3,2,1,0:T(8,128)S(1)}, u32[]{:S(2)}) copy-start(f32[1,16,32,256]{3,2,1,0:T(8,128)S(1)} %fusion.25) | copy-start | bytes 1572868
  1887.3 4.3 collective-permute-start.16
  1889.3 8.8 collective-permute-start.17
  1898.1 5.9 collective-permute-start.18
  1900.1 7.8 collective-permute-start.19
  (13 other events, 94.7 us)
Sparse Core Ops, SparseCore 0:
  55.6 375.8 all-reduce.6
  1383.0 70.3 reduce-scatter.1
where the time goes:
time: 1950 us; the launch traced here: 1920 us
  local copies, waits for them, and re-layouts  977 us (50%)
  waiting for transfers between devices  445 us (23%)
  blocking collectives  299 us (15%)
  other arithmetic  113 us (6%)
  starting transfers between devices  63.2 us (3%)
    gather x2, local copies, waits for them, and re-layouts, body(): sampled = flat_inflow[:, sample_cells]  946 us
    psum x1, waiting for transfers between devices, broadcast(): return lax.psum(kept, axis)  373 us
    all_gather x1, blocking collectives, body(): gathered = lax.all_gather(forces, ('slab', 'cross'), axis=1, tiled=True)  269 us
    scatter-add x1, other arithmetic, body(): jnp.zeros((3, cells_y * cells_z), jnp.float32).at[:, force_cell].add(pushed)  81.9 us
    reduce_scatter x1, waiting for transfers between devices, body(): lax.psum_scatter(jnp.dot(inv_influence, normal_flow, preferred_element_ty...  39.3 us
  transfers between devices with their start and end apart: 22, of which 8 were waited for; matrix products, arithmetic and copies ran while one was open for 6% of the time, Pallas kernels for 0%

commit v1 on v0

v1 whole, which is shorter than its diff:
```python
import functools

import jax
import jax.numpy as jnp
from jax import lax
from jax.experimental import pallas as pl
from jax.experimental.pallas import tpu as pltpu
from jax.sharding import PartitionSpec as P

MESH = pl.DeviceIdType.MESH
F32 = jnp.float32
BF16 = jnp.bfloat16
SIXTH = 1.0 / 6.0
CHUNKS = 4
GROUP = 4


def z_next(a):
    lane = lax.broadcasted_iota(jnp.int32, a.shape, 1)
    return jnp.where(lane == 255, 0.0, pltpu.roll(a, 255, 1))


def z_prev(a):
    lane = lax.broadcasted_iota(jnp.int32, a.shape, 1)
    return jnp.where(lane == 0, 0.0, pltpu.roll(a, 1, 1))


def y_next(a, edge):
    n = a.shape[0]
    row = lax.broadcasted_iota(jnp.int32, a.shape, 0)
    return jnp.where(row == n - 1, edge, pltpu.roll(a, n - 1, 0))


def y_prev(a, edge):
    n = a.shape[0]
    row = lax.broadcasted_iota(jnp.int32, a.shape, 0)
    return jnp.where(row == 0, edge, pltpu.roll(a, 1, 0))


def kernel(
    vel, pres, inv, nrm, cells, tang, owner, cell,
    vel_out, pres_out,
    V, P0, PR, P1, P2, DV, OV,
    EDGE_S, EDGE_R,
    PL, T, A, CI, ZB, YH, YL, NS, TG, KO, KC, RK, ZK,
    NFS, NF, NFB, SB, RB1, SB2, RB2, FB, FA, LHS, RHS, ACC,
    load_sem, ns_sem, a1s, a1r, a2s, a2r, a3s, a3r, ns, nr, e1s, e1r, e2s, e2r,
    f1s, f1r, f2s, f2r, xs, xr, ys, yr, out_sem,
):
    slab = lax.axis_index("slab")
    cross = lax.axis_index("cross")
    h = lax.rem(slab, 2)
    chip = slab // 2
    sib = slab + 1 - 2 * h

    def remote(src, dst, ss, rs, s, c):
        return pltpu.make_async_remote_copy(
            src_ref=src, dst_ref=dst, send_sem=ss, recv_sem=rs, device_id=(s, c), device_id_type=MESH
        )

    def cr(d):
        return lax.rem(cross + d, 8)

    def sl(d):
        return lax.rem(slab + d, 16)

    loads = [
        pltpu.make_async_copy(vel, V.at[:, pl.ds(1, 16)], load_sem.at[0]),
        pltpu.make_async_copy(pres, P0.at[pl.ds(1, 16)], load_sem.at[1]),
        pltpu.make_async_copy(cells.at[pl.ds(pl.multiple_of(cross * 128, 128), 128)], CI, load_sem.at[2]),
        pltpu.make_async_copy(nrm.at[cross], NS, load_sem.at[3]),
        pltpu.make_async_copy(inv, A, load_sem.at[4]),
        pltpu.make_async_copy(tang, TG, load_sem.at[5]),
        pltpu.make_async_copy(owner, KO, load_sem.at[6]),
        pltpu.make_async_copy(cell, KC, load_sem.at[7]),
    ]
    for load in loads:
        load.start()

    barrier = pltpu.get_barrier_semaphore()
    for d in range(1, 16):
        pl.semaphore_signal(barrier, inc=1, device_id=(sl(d), cross), device_id_type=MESH)
    for d in range(1, 8):
        pl.semaphore_signal(barrier, inc=1, device_id=(slab, cr(d)), device_id_type=MESH)
    pl.semaphore_wait(barrier, 22)

    def a1_copy(target):
        half = target % 2
        return remote(
            vel.at[:, 8, pl.ds(half * 16, 16)],
            PL.at[:, pl.ds(pl.multiple_of(cross * 32 + half * 16, 16), 16)],
            a1s.at[target], a1r.at[0], target, cross,
        )

    def tile(c, half):
        return PL.at[:, pl.ds(pl.multiple_of(c * 32 + half * 16, 16), 16)]

    others = [t for t in (6, 8, 5, 4, 9, 2, 1, 3, 0, 10, 14, 15, 11, 13, 12)]

    @pl.when(slab == 7)
    def _():
        for t in others:
            a1_copy(t).start()
        own = pltpu.make_async_copy(vel.at[:, 8, pl.ds(16, 16)], tile(cross, 1), a1r.at[0])
        own.start()

    def x_pair(src_hi, dst_lo, src_lo, dst_hi, k):
        up = remote(src_hi, dst_lo, xs.at[k, 0], xr.at[k, 0], sl(1), cross)
        down = remote(src_lo, dst_hi, xs.at[k, 1], xr.at[k, 1], sl(15), cross)
        return up, down

    def y_pair(k):
        up = remote(EDGE_S.at[k, 0], EDGE_R.at[k, 0], ys.at[k, 0], yr.at[k, 0], slab, cr(1))
        down = remote(EDGE_S.at[k, 1], EDGE_R.at[k, 1], ys.at[k, 1], yr.at[k, 1], slab, cr(7))
        return up, down

    pairs = [x_pair(vel.at[:, 15], V.at[:, 0], vel.at[:, 0], V.at[:, 17], 0),
             x_pair(pres.at[15], P0.at[0], pres.at[0], P0.at[17], 1)]
    for pair in pairs:
        for copy in pair:
            copy.start()

    loads[0].wait()
    loads[1].wait()

    def fill_edges(k, source):
        def step(x, _):
            EDGE_S[k, 0, pl.ds(x, 1), :] = source(x, 31)
            EDGE_S[k, 1, pl.ds(x, 1), :] = source(x, 0)
            return 0
        lax.fori_loop(0, 16, step, 0)

    for i in range(3):
        fill_edges(i, lambda x, r, i=i: V[i, x + 1, r:r + 1, :])
    fill_edges(3, lambda x, r: P0[x + 1, r:r + 1, :])
    v_edges = [y_pair(k) for k in range(4)]
    for pair in v_edges:
        for copy in pair:
            copy.start()

    def finish(pair):
        for copy in pair:
            copy.wait_recv()

    def clear_planes(refs):
        @pl.when(slab == 0)
        def _():
            for ref, lo, hi in refs:
                lo[...] = jnp.zeros(lo.shape, F32)

        @pl.when(slab == 15)
        def _():
            for ref, lo, hi in refs:
                hi[...] = jnp.zeros(hi.shape, F32)

    def clear_rows(ks):
        @pl.when(cross == 0)
        def _():
            for k in ks:
                EDGE_R[k, 0] = jnp.zeros((16, 256), F32)

        @pl.when(cross == 7)
        def _():
            for k in ks:
                EDGE_R[k, 1] = jnp.zeros((16, 256), F32)

    loads[2].wait()
    ci = CI[...]
    ZB[...] = (ci & 255).astype(F32)
    YH[...] = (ci >> 15).astype(F32)
    YL[...] = (ci >> 8) & 127

    a1_in = remote(vel.at[:, 8, pl.ds(0, 16)], tile(cross, h), a1s.at[0], a1r.at[0], slab, cross)
    a1_in.wait_recv()
    a2 = [None] + [
        remote(tile(cross, h), tile(cross, h), a2s.at[d], a2r.at[d], slab, cr(d)) for d in range(1, 8)
    ]
    for d in (4, 1, 7, 3, 5, 2, 6):
        a2[d].start()

    def a3_copy(d):
        src = tile(cr(8 - d), h)
        return remote(src, src, a3s.at[d], a3r.at[d], sib, cross)

    a3_copy(0).start()

    for pair in pairs:
        finish(pair)
    for pair in v_edges:
        finish(pair)
    clear_planes([(V, V.at[:, 0], V.at[:, 17]), (P0, P0.at[0], P0.at[17])])
    clear_rows(range(4))

    def around(u, lo, hi, k, x):
        mid = u(x + 1)
        s = u(x + 2) + u(x)
        s = s + y_next(mid, EDGE_R[k, 1, pl.ds(x, 1), :]) + y_prev(mid, EDGE_R[k, 0, pl.ds(x, 1), :])
        return s + z_next(mid) + z_prev(mid)

    def predict(x, _):
        for i in range(3):
            mid = V[i, x + 1]
            s = around(lambda q: V[i, q], None, None, i, x)
            pr = mid + 0.5 * (0.1 * (s - 6.0 * mid))
            PR[i, x + 1] = pr
            if i == 1:
                EDGE_S[4, 0, pl.ds(x, 1), :] = pr[31:32, :]
                EDGE_S[4, 1, pl.ds(x, 1), :] = pr[0:1, :]
        return 0

    lax.fori_loop(0, 16, predict, 0)
    pr_x = x_pair(PR.at[0, 16], PR.at[0, 0], PR.at[0, 1], PR.at[0, 17], 2)
    pr_y = y_pair(4)
    for copy in pr_x + pr_y:
        copy.start()

    for d in (1, 7, 4, 3, 5, 2, 6):
        remote(tile(cross, h), tile(cr(8 - d), h), a2s.at[d], a2r.at[d], slab, cross).wait_recv()
        a3_copy(d).start()

    finish(pr_x)
    finish(pr_y)
    clear_planes([(PR, PR.at[0, 0], PR.at[0, 17])])
    clear_rows([4])

    def diverge(x, _):
        py = PR[1, x + 1]
        pz = PR[2, x + 1]
        g = PR[0, x + 2] - PR[0, x]
        g = g + (y_next(py, EDGE_R[4, 1, pl.ds(x, 1), :]) - y_prev(py, EDGE_R[4, 0, pl.ds(x, 1), :]))
        g = 0.5 * (g + (z_next(pz) - z_prev(pz)))
        DV[x] = g
        p = (around(lambda q: P0[q], None, None, 3, x) - g) * SIXTH
        P1[x + 1] = p
        EDGE_S[5, 0, pl.ds(x, 1), :] = p[31:32, :]
        EDGE_S[5, 1, pl.ds(x, 1), :] = p[0:1, :]
        return 0

    lax.fori_loop(0, 16, diverge, 0)
    p1_x = x_pair(P1.at[16], P1.at[0], P1.at[1], P1.at[17], 3)
    p1_y = y_pair(5)
    for copy in p1_x + p1_y:
        copy.start()

    for d in (0, 1, 7, 4, 3, 5, 2, 6):
        remote(tile(cross, h), tile(cr(8 - d), 1 - h), a3s.at[d], a3r.at[d], sib, cross).wait_recv()
    for c in range(3):
        for k in range(2):
            T[pl.ds(c * 128, 128), pl.ds(k * 256, 256)] = PL[c, pl.ds(k * 128, 128), :].astype(BF16)

    loads[3].wait()

    row16 = lax.broadcasted_iota(jnp.int32, (16, 16, 256), 0) * 16 + lax.broadcasted_iota(jnp.int32, (16, 16, 256), 1)
    z_of = row16.astype(F32).astype(BF16)
    y_of = lax.broadcasted_iota(jnp.int32, (16, 8, 256), 0) * 8 + lax.broadcasted_iota(jnp.int32, (16, 8, 256), 1)
    rows = 128 // CHUNKS

    def lookup(j):
        zb = jnp.broadcast_to(ZB[pl.ds(j, 1), :], (16, 256)).astype(BF16)[None]
        yh = jnp.broadcast_to(YH[pl.ds(j, 1), :], (16, 256)).astype(BF16)[None]
        mask = z_of == zb
        zero = jnp.zeros((16, 16, 256), BF16)
        one = jnp.ones((1, 16, 256), BF16)
        hot = jnp.concatenate(
            [jnp.where(mask, one - yh, zero).reshape(256, 256), jnp.where(mask, yh, zero).reshape(256, 256)], axis=0
        )
        r = jnp.dot(T[...], hot, preferred_element_type=F32).reshape(3, 16, 8, 256)
        ym = y_of == jnp.broadcast_to(YL[pl.ds(j, 1), :], (8, 256))[None]
        acc = NS[0, j] * jnp.sum(jnp.where(ym, r[0], 0.0), axis=0)
        acc = acc + NS[1, j] * jnp.sum(jnp.where(ym, r[1], 0.0), axis=0)
        acc = acc + NS[2, j] * jnp.sum(jnp.where(ym, r[2], 0.0), axis=0)
        NFS[pl.ds(j, 1), :] = jnp.sum(acc, axis=0, keepdims=True).astype(BF16).astype(F32)

    def nf_copy(d, k):
        part = pl.ds(k * rows, rows)
        return remote(NFS.at[part], NF.at[cross, part], ns.at[d, k], nr.at[d, k], slab, cr(d))

    for k in range(CHUNKS):
        def look(i, _):
            for g in range(GROUP):
                lookup(k * rows + i * GROUP + g)
            return 0
        lax.fori_loop(0, rows // GROUP, look, 0)
        for d in (4, 1, 7, 3, 5, 2, 6):
            nf_copy(d, k).start()

    finish(p1_x)
    finish(p1_y)
    clear_planes([(P1, P1.at[0], P1.at[17])])
    clear_rows([5])

    def sweep(x, _):
        p = (around(lambda q: P1[q], None, None, 5, x) - DV[x]) * SIXTH
        P2[x + 1] = p
        EDGE_S[6, 0, pl.ds(x, 1), :] = p[31:32, :]
        EDGE_S[6, 1, pl.ds(x, 1), :] = p[0:1, :]
        return 0

    lax.fori_loop(0, 16, sweep, 0)
    p2_x = x_pair(P2.at[16], P2.at[0], P2.at[1], P2.at[17], 4)
    p2_y = y_pair(6)
    for copy in p2_x + p2_y:
        copy.start()

    NFB[cross] = NFS[...].astype(BF16)
    for d in range(1, 8):
        src = cr(8 - d)
        for k in range(CHUNKS):
            part = pl.ds(k * rows, rows)
            remote(NFS.at[part], NF.at[src, part], ns.at[d, k], nr.at[d, k], slab, cross).wait_recv()
        NFB[src] = NF[src].astype(BF16)

    loads[4].wait()
    groups = ((1, 2, 3, 4), (5, 6, 7, 0))

    def partial(ds, half):
        lhs = jnp.concatenate([A[lax.rem(chip + d, 8), half] for d in ds], axis=0)
        return jnp.dot(lhs, NFB[...].reshape(1024, 256), preferred_element_type=F32)

    def e1_copy(d):
        return remote(SB.at[d], RB1.at[d], e1s.at[d], e1r.at[d], sib, cross)

    def e2_copy(d):
        return remote(SB2.at[d], RB2.at[d], e2s.at[d], e2r.at[d], lax.rem(chip + d, 8) * 2 + h, cross)

    for ds in groups:
        p = partial(ds, 1 - h)
        for n, d in enumerate(ds):
            SB[d] = p[n * 128:(n + 1) * 128]
            e1_copy(d).start()
    for ds in groups:
        p = partial(ds, h)
        for n, d in enumerate(ds):
            e1_copy(d).wait_recv()
            SB2[d] = p[n * 128:(n + 1) * 128] + RB1[d]
            if d:
                e2_copy(d).start()

    finish(p2_x)
    finish(p2_y)
    clear_planes([(P2, P2.at[0], P2.at[17])])
    clear_rows([6])

    def correct(x, _):
        mid = P2[x + 1]
        OV[0, x] = PR[0, x + 1] - 0.5 * (P2[x + 2] - P2[x])
        gy = y_next(mid, EDGE_R[6, 1, pl.ds(x, 1), :]) - y_prev(mid, EDGE_R[6, 0, pl.ds(x, 1), :])
        OV[1, x] = PR[1, x + 1] - 0.5 * gy
        OV[2, x] = PR[2, x + 1] - 0.5 * (z_next(mid) - z_prev(mid))
        return 0

    lax.fori_loop(0, 16, correct, 0)

    def outs(k, lo, n):
        return [
            pltpu.make_async_copy(OV.at[:, pl.ds(lo, n)], vel_out.at[:, pl.ds(lo, n)], out_sem.at[2 * k]),
            pltpu.make_async_copy(P2.at[pl.ds(lo + 1, n)], pres_out.at[pl.ds(lo, n)], out_sem.at[2 * k + 1]),
        ]

    early = outs(0, 4, 8)
    late = outs(1, 0, 4) + outs(2, 12, 4)
    for copy in early:
        copy.start()

    loads[6].wait()
    loads[7].wait()
    ko = KO[...]
    kc = KC[...]
    rel = (ko & 7) * 32 + (kc >> 8) - (cross * 32 - 4)
    RK[...] = jnp.where((rel >= 0) & (rel < 40), (ko >> 3) * 40 + rel, -1).astype(F32)
    ZK[...] = (kc & 255).astype(F32)

    loads[5].wait()
    total = SB2[0]
    for d in range(1, 8):
        e2_copy(d).wait_recv()
        total = total + RB2[d]
    mean = lax.dot_general(
        jnp.ones((8, 256), F32), total * total, (((1,), (1,)), ((), ())),
        precision=lax.Precision.HIGHEST, preferred_element_type=F32,
    )[0:1] * (1.0 / 256.0)
    FB[...] = TG[...] * mean

    def f1_copy(k):
        return remote(FB, FA.at[cross, slab], f1s.at[k], f1r.at[slab], 7 + k, cross)

    for k in range(2):
        @pl.when(slab != 7 + k)
        def _():
            f1_copy(k).start()

    @pl.when((slab == 7) | (slab == 8))
    def _():
        FA[cross, slab] = FB[...]
        for s in range(16):
            @pl.when(slab != s)
            def _():
                remote(FB, FA.at[cross, s], f1s.at[0], f1r.at[s], slab, cross).wait_recv()

        f2 = [remote(FA.at[cross], FA.at[cross], f2s.at[d], f2r.at[d], slab, cr(d)) for d in range(1, 8)]
        for copy in f2:
            copy.start()

        for d in range(1, 8):
            src = FA.at[cr(8 - d)]
            remote(src, src, f2s.at[d], f2r.at[d], slab, cross).wait_recv()

        r_of = (lax.broadcasted_iota(jnp.int32, (5, 16, 128), 0) * 16
                + lax.broadcasted_iota(jnp.int32, (5, 16, 128), 1)).astype(F32).astype(BF16)
        z_at = (lax.broadcasted_iota(jnp.int32, (16, 16, 128), 0) * 16
                + lax.broadcasted_iota(jnp.int32, (16, 16, 128), 1)).astype(F32).astype(BF16)
        ACC[...] = jnp.zeros(ACC.shape, F32)

        def add(c, _):
            for s in range(16):
                q = c * 16 + s
                lanes = pl.ds(s * 128, 128)
                rk = jnp.broadcast_to(RK[pl.ds(q, 1), :], (16, 128)).astype(BF16)[None]
                zk = jnp.broadcast_to(ZK[pl.ds(q, 1), :], (16, 128)).astype(BF16)[None]
                f = FA[c, s]
                hi = f.astype(BF16).astype(F32)
                lo = f - hi
                mask = r_of == rk
                for i in range(3):
                    for n, part in enumerate((hi, lo)):
                        value = jnp.broadcast_to(part[i:i + 1], (16, 128)).astype(BF16)[None]
                        LHS[pl.ds((i * 2 + n) * 5, 5), :, lanes] = jnp.where(mask, value, jnp.zeros((5, 16, 128), BF16))
                RHS[:, :, lanes] = jnp.where(z_at == zk, jnp.ones((1, 16, 128), BF16), jnp.zeros((16, 16, 128), BF16))
            ACC[...] += lax.dot_general(
                LHS[...].reshape(480, 2048), RHS[...].reshape(256, 2048), (((1,), (1,)), ((), ())),
                preferred_element_type=F32,
            )
            return 0

        lax.fori_loop(0, 8, add, 0)

        push = {}
        for i in range(3):
            for p in range(2):
                at = i * 160 + p * 40
                push[i, 127 + p] = 0.5 * (ACC[at:at + 40, :] + ACC[at + 80:at + 120, :])
        row = lax.broadcasted_iota(jnp.int32, (40, 256), 0) + (cross * 32 - 4)
        inside = (row >= 0) & (row < 256)

        def within(a):
            return jnp.where(inside, a, 0.0)

        def ny(a):
            return pltpu.roll(a, 39, 0)

        def py(a):
            return pltpu.roll(a, 1, 0)

        div = {126: 0.5 * push[0, 127], 129: -0.5 * push[0, 128]}
        for x, side in ((127, push[0, 128]), (128, -push[0, 127])):
            a, b = push[1, x], push[2, x]
            div[x] = within(0.5 * (side + (ny(a) - py(a)) + (z_next(b) - z_prev(b))))
        one = {x: -SIXTH * div[x] for x in div}
        two = {}
        for x in range(125, 131):
            s = None
            if x in one:
                a = one[x]
                s = ny(a) + py(a) + z_next(a) + z_prev(a) - div[x]
            for near in (x - 1, x + 1):
                if near in one:
                    s = one[near] if s is None else s + one[near]
            two[x] = within(s * SIXTH)

        def centre(a):
            return pltpu.roll(a, 36, 0)[0:32]

        def apply(first, local):
            for n in range(4):
                x = first + n
                g = None
                if x + 1 in two:
                    g = two[x + 1]
                if x - 1 in two:
                    g = -two[x - 1] if g is None else g - two[x - 1]
                vx = -0.5 * g
                if x in (127, 128):
                    vx = vx + push[0, x]
                OV[0, local + n] += centre(vx)
                if x in two:
                    a = two[x]
                    P2[local + n + 1] += centre(a)
                    vy = -0.5 * (ny(a) - py(a))
                    vz = -0.5 * (z_next(a) - z_prev(a))
                    if x in (127, 128):
                        vy = vy + push[1, x]
                        vz = vz + push[2, x]
                    OV[1, local + n] += centre(vy)
                    OV[2, local + n] += centre(vz)

        for copy in p2_x:
            copy.wait_send()

        @pl.when(slab == 7)
        def _():
            apply(124, 12)

        @pl.when(slab == 8)
        def _():
            apply(128, 0)

        for copy in f2:
            copy.wait_send()

    for copy in late:
        copy.start()

    @pl.when(slab == 7)
    def _():
        for t in others:
            a1_copy(t).wait_send()
    for d in range(8):
        if d:
            a2[d].wait_send()
            for k in range(CHUNKS):
                nf_copy(d, k).wait_send()
            e2_copy(d).wait_send()
        a3_copy(d).wait_send()
        e1_copy(d).wait_send()
    for pair in pairs + v_edges + [pr_x, pr_y, p1_x, p1_y, p2_y]:
        for copy in pair:
            copy.wait_send()

    @pl.when((slab != 7) & (slab != 8))
    def _():
        for copy in p2_x:
            copy.wait_send()
    for k in range(2):
        @pl.when(slab != 7 + k)
        def _():
            f1_copy(k).wait_send()
    for copy in early + late:
        copy.wait()


def body(velocity, pressure, inv_influence, normals, sample_cells, tangents, force_owner, force_cell):
    any_space = pl.BlockSpec(memory_space=pl.ANY)
    dma = pltpu.SemaphoreType.DMA
    vm = pltpu.VMEM
    return pl.pallas_call(
        kernel,
        out_shape=(
            jax.ShapeDtypeStruct(velocity.shape, F32),
            jax.ShapeDtypeStruct(pressure.shape, F32),
        ),
        in_specs=[any_space] * 8,
        out_specs=(any_space, any_space),
        scratch_shapes=[
            vm((3, 18, 32, 256), F32), vm((18, 32, 256), F32), vm((3, 18, 32, 256), F32),
            vm((18, 32, 256), F32), vm((18, 32, 256), F32), vm((16, 32, 256), F32), vm((3, 16, 32, 256), F32),
            vm((7, 2, 16, 256), F32), vm((7, 2, 16, 256), F32),
            vm((3, 256, 256), F32), vm((384, 512), BF16), vm((8, 2, 128, 1024), BF16), vm((128, 256), jnp.int32),
            vm((128, 256), F32), vm((128, 256), F32), vm((128, 256), jnp.int32),
            pltpu.SMEM((3, 128), F32), vm((3, 128), F32),
            vm((128, 128), jnp.int32), vm((128, 128), jnp.int32), vm((128, 128), F32), vm((128, 128), F32),
            vm((128, 256), F32), vm((8, 128, 256), F32), vm((8, 128, 256), BF16),
            vm((8, 128, 256), F32), vm((8, 128, 256), F32), vm((8, 128, 256), F32), vm((8, 128, 256), F32),
            vm((3, 128), F32), vm((8, 16, 3, 128), F32),
            vm((30, 16, 2048), BF16), vm((16, 16, 2048), BF16), vm((480, 256), F32),
            dma((8,)), dma((1,)), dma((16,)), dma((1,)), dma((8,)), dma((8,)), dma((8,)), dma((8,)),
            dma((8, CHUNKS)), dma((8, CHUNKS)), dma((8,)), dma((8,)), dma((8,)), dma((8,)),
            dma((2,)), dma((16,)), dma((8,)), dma((8,)), dma((5, 2)), dma((5, 2)), dma((7, 2)), dma((7, 2)),
            dma((6,)),
        ],
        compiler_params=pltpu.CompilerParams(
            collective_id=0, has_side_effects=True, vmem_limit_bytes=56 * 1024 * 1024
        ),
    )(
        velocity, pressure, inv_influence.reshape(8, 2, 128, 1024),
        normals.reshape(3, 8, 128).transpose(1, 0, 2), sample_cells, tangents.reshape(3, 128),
        force_owner.reshape(128, 128), force_cell.reshape(128, 128),
    )


def solution(mesh):
    return jax.shard_map(
        body,
        mesh=mesh,
        in_specs=(
            P(None, "slab", "cross", None),
            P("slab", "cross", None),
            P("cross", "slab"),
            P(None, "slab"),
            P("slab", None),
            P(None, "cross", "slab", None),
            P(),
            P(),
        ),
        out_specs=(P(None, "slab", "cross", None), P("slab", "cross", None)),
        check_vma=False,
    )
```

time: 1950 us -> 94.7 us (0.05); the launches traced: 1920 us -> 94.2 us
  local copies, waits for them, and re-layouts: 977 us -> 4.84 us
  waiting for transfers between devices: 445 us -> 0 us
  blocking collectives: 299 us -> 0 us
  other arithmetic: 113 us -> 0 us
  Pallas kernels: 0 us -> 88.7 us
  starting transfers between devices: 63.2 us -> 0 us
    gather x2 -> x0, local copies, waits for them, and re-layouts: 946 us -> none  [body(): sampled = flat_inflow[:, sample_cells]]
    psum x1 -> x0, waiting for transfers between devices: 373 us -> none  [broadcast(): return lax.psum(kept, axis)]
    all_gather x2 -> x0, blocking collectives: 299 us -> none  [the longest x1 269 us: body(): gathered = lax.all_gather(forces, ('slab', 'cross'), axis=1, tiled=True)]
    pallas_call x0 -> x1, Pallas kernels: none -> 88.7 us  [body(): pl.pallas_call(kernel, out_shape=(jax.ShapeDtypeStruct(velocity.shape, F3...]
    scatter-add x1 -> x0, other arithmetic: 81.9 us -> none  [body(): jnp.zeros((3, cells_y * cells_z), jnp.float32).at[:, force_cell].add(pushed)]
    ppermute x20 -> x0, starting transfers between devices: 63.1 us -> none  [the longest x10 38.3 us: padded_2(): lax.ppermute(lax.slice_in_dim(block, 0, width, axis=dim), axis, backward)]
    reduce_scatter x1 -> x0, waiting for transfers between devices: 39.3 us -> none  [body(): lax.psum_scatter(jnp.dot(inv_influence, normal_flow, preferred_element_ty...]
    ppermute x20 -> x0, waiting for transfers between devices: 32.1 us -> none  [the longest x10 32.1 us: padded_2(): lax.ppermute(lax.slice_in_dim(block, block.shape[dim] - width, None, axis...]
  transfers between devices with their start and end apart: 22 -> 0, of which waited for: 8 -> 0; matrix products, arithmetic and copies ran while one was open for 6% -> 0% of each run, Pallas kernels for 0% -> 0%
where the time goes in v1:
time: 94.7 us; the launch traced here: 94.2 us
  Pallas kernels  88.7 us (94%)
  local copies, waits for them, and re-layouts  4.84 us (5%)
    pallas_call x1, Pallas kernels, body(): pl.pallas_call(kernel, out_shape=(jax.ShapeDtypeStruct(velocity.shape, F3...  88.7 us
    unnamed x5, local copies, waits for them, and re-layouts  4.84 us

profile of v1, /device:TPU:6, one launch (start us, length us, event | category | flops | bytes accessed | tf_op | source)
XLA Modules:
  0.0 94.2 jit_solution(5666136360374415117)
XLA Ops:
  0.6 1.3 %copy.12 = f32[3,1,1,128]{3,0,1,2:T(4,128)} copy(f32[3,1,1,128]{3,2,1,0:T(1,128)} %param.13) | data formatting | bytes 3072
  1.9 88.7 %shard_map.95 = (f32[3,16,32,256]{3,2,1,0:T(8,128)}, f32[16,32,256]{2,1,0:T(8,128)}) custom-call(f32[3,16,32,256]{3,2,1,0:T(8,128)} %vel.1, f32[16,32,256]{2,1,0:T(8,128)} %pres.1, bf16[8,2,128,1024]{3,2,1,0:T(8,128)(2,1)} %bitcast.9, f32[8,3,128]{2,1,0:T(4,128)} %bitcast.12, s32[1024,256]{1,0:T(8,128)} %cells.1, f32[3,128]{1,0:T(4,128)} %bitcast.13, ...), custom_call_target="tpu_custom_call" | custom-call | tf_op jit(solution)/shard_map/pallas_call | solution.py:545
  90.6 0.0 copy-start
  90.6 2.8 %copy.15 = f32[3,16,32,256]{3,2,1,0:T(8,128)} copy(f32[3,16,32,256]{3,2,1,0:T(8,128)} %get-tuple-element.4) | data formatting | bytes 3145728
  93.4 0.0 copy-done
  93.4 0.8 copy.16
Async XLA Ops:
  90.6 2.8 %copy-start = (f32[16,32,256]{2,1,0:T(8,128)S(1)}, f32[16,32,256]{2,1,0:T(8,128)}, u32[]{:S(2)}) copy-start(f32[16,32,256]{2,1,0:T(8,128)} %get-tuple-element.5) | copy-start | bytes 1572868

commit v2 on v1

--- a/solution.py
+++ b/solution.py
@@ -12,7 +12,7 @@
 BF16 = jnp.bfloat16
 SIXTH = 1.0 / 6.0
 CHUNKS = 4
-GROUP = 4
+GROUP = 16
 
 
 def z_next(a):
@@ -39,13 +39,13 @@
 
 def kernel(
     vel, pres, inv, nrm, cells, tang, owner, cell,
-    vel_out, pres_out,
+    ov_out, p2_out, push_out,
     V, P0, PR, P1, P2, DV, OV,
     EDGE_S, EDGE_R,
     PL, T, A, CI, ZB, YH, YL, NS, TG, KO, KC, RK, ZK,
-    NFS, NF, NFB, SB, RB1, SB2, RB2, FB, FA, LHS, RHS, ACC,
+    NFS, NF, NFB, SB, RB1, SB2, RB2, FB, FA, LHS, RHS, ACC, PUSH,
     load_sem, ns_sem, a1s, a1r, a2s, a2r, a3s, a3r, ns, nr, e1s, e1r, e2s, e2r,
-    f1s, f1r, f2s, f2r, xs, xr, ys, yr, out_sem,
+    f1s, f1r, xs, xr, ys, yr, out_sem,
 ):
     slab = lax.axis_index("slab")
     cross = lax.axis_index("cross")
@@ -103,6 +103,8 @@
             a1_copy(t).start()
         own = pltpu.make_async_copy(vel.at[:, 8, pl.ds(16, 16)], tile(cross, 1), a1r.at[0])
         own.start()
+        for t in others:
+            a1_copy(t).wait_send()
 
     def x_pair(src_hi, dst_lo, src_lo, dst_hi, k):
         up = remote(src_hi, dst_lo, xs.at[k, 0], xr.at[k, 0], sl(1), cross)
@@ -169,6 +171,28 @@
     ZB[...] = (ci & 255).astype(F32)
     YH[...] = (ci >> 15).astype(F32)
     YL[...] = (ci >> 8) & 127
+
+    loads[6].wait()
+    loads[7].wait()
+    ko = KO[...]
+    kc = KC[...]
+    rel = (ko & 7) * 32 + (kc >> 8) - (cross * 32 - 4)
+    RK[...] = jnp.where((rel >= 0) & (rel < 40), (ko >> 3) * 40 + rel, -1).astype(F32)
+    ZK[...] = (kc & 255).astype(F32)
+
+    z_at = (lax.broadcasted_iota(jnp.int32, (16, 16, 128), 0) * 16
+            + lax.broadcasted_iota(jnp.int32, (16, 16, 128), 1)).astype(F32).astype(BF16)
+
+    @pl.when((slab == 7) | (slab == 8))
+    def _():
+        def place(c, _):
+            for s in range(16):
+                zk = jnp.broadcast_to(ZK[pl.ds(c * 16 + s, 1), :], (16, 128)).astype(BF16)[None]
+                RHS[c, :, :, s * 128:(s + 1) * 128] = jnp.where(
+                    z_at == zk, jnp.ones((1, 16, 128), BF16), jnp.zeros((16, 16, 128), BF16)
+                )
+            return 0
+        lax.fori_loop(0, 8, place, 0)
 
     a1_in = remote(vel.at[:, 8, pl.ds(0, 16)], tile(cross, h), a1s.at[0], a1r.at[0], slab, cross)
     a1_in.wait_recv()
@@ -217,30 +241,6 @@
     for d in (1, 7, 4, 3, 5, 2, 6):
         remote(tile(cross, h), tile(cr(8 - d), h), a2s.at[d], a2r.at[d], slab, cross).wait_recv()
         a3_copy(d).start()
-
-    finish(pr_x)
-    finish(pr_y)
-    clear_planes([(PR, PR.at[0, 0], PR.at[0, 17])])
-    clear_rows([4])
-
-    def diverge(x, _):
-        py = PR[1, x + 1]
-        pz = PR[2, x + 1]
-        g = PR[0, x + 2] - PR[0, x]
-        g = g + (y_next(py, EDGE_R[4, 1, pl.ds(x, 1), :]) - y_prev(py, EDGE_R[4, 0, pl.ds(x, 1), :]))
-        g = 0.5 * (g + (z_next(pz) - z_prev(pz)))
-        DV[x] = g
-        p = (around(lambda q: P0[q], None, None, 3, x) - g) * SIXTH
-        P1[x + 1] = p
-        EDGE_S[5, 0, pl.ds(x, 1), :] = p[31:32, :]
-        EDGE_S[5, 1, pl.ds(x, 1), :] = p[0:1, :]
-        return 0
-
-    lax.fori_loop(0, 16, diverge, 0)
-    p1_x = x_pair(P1.at[16], P1.at[0], P1.at[1], P1.at[17], 3)
-    p1_y = y_pair(5)
-    for copy in p1_x + p1_y:
-        copy.start()
 
     for d in (0, 1, 7, 4, 3, 5, 2, 6):
         remote(tile(cross, h), tile(cr(8 - d), 1 - h), a3s.at[d], a3r.at[d], sib, cross).wait_recv()
@@ -284,22 +284,28 @@
         for d in (4, 1, 7, 3, 5, 2, 6):
             nf_copy(d, k).start()
 
-    finish(p1_x)
-    finish(p1_y)
-    clear_planes([(P1, P1.at[0], P1.at[17])])
-    clear_rows([5])
-
-    def sweep(x, _):
-        p = (around(lambda q: P1[q], None, None, 5, x) - DV[x]) * SIXTH
-        P2[x + 1] = p
-        EDGE_S[6, 0, pl.ds(x, 1), :] = p[31:32, :]
-        EDGE_S[6, 1, pl.ds(x, 1), :] = p[0:1, :]
+    finish(pr_x)
+    finish(pr_y)
+    clear_planes([(PR, PR.at[0, 0], PR.at[0, 17])])
+    clear_rows([4])
+
+    def diverge(x, _):
+        py = PR[1, x + 1]
+        pz = PR[2, x + 1]
+        g = PR[0, x + 2] - PR[0, x]
+        g = g + (y_next(py, EDGE_R[4, 1, pl.ds(x, 1), :]) - y_prev(py, EDGE_R[4, 0, pl.ds(x, 1), :]))
+        g = 0.5 * (g + (z_next(pz) - z_prev(pz)))
+        DV[x] = g
+        p = (around(lambda q: P0[q], None, None, 3, x) - g) * SIXTH
+        P1[x + 1] = p
+        EDGE_S[5, 0, pl.ds(x, 1), :] = p[31:32, :]
+        EDGE_S[5, 1, pl.ds(x, 1), :] = p[0:1, :]
         return 0
 
-    lax.fori_loop(0, 16, sweep, 0)
-    p2_x = x_pair(P2.at[16], P2.at[0], P2.at[1], P2.at[17], 4)
-    p2_y = y_pair(6)
-    for copy in p2_x + p2_y:
+    lax.fori_loop(0, 16, diverge, 0)
+    p1_x = x_pair(P1.at[16], P1.at[0], P1.at[1], P1.at[17], 3)
+    p1_y = y_pair(5)
+    for copy in p1_x + p1_y:
         copy.start()
 
     NFB[cross] = NFS[...].astype(BF16)
@@ -336,6 +342,24 @@
             if d:
                 e2_copy(d).start()
 
+    finish(p1_x)
+    finish(p1_y)
+    clear_planes([(P1, P1.at[0], P1.at[17])])
+    clear_rows([5])
+
+    def sweep(x, _):
+        p = (around(lambda q: P1[q], None, None, 5, x) - DV[x]) * SIXTH
+        P2[x + 1] = p
+        EDGE_S[6, 0, pl.ds(x, 1), :] = p[31:32, :]
+        EDGE_S[6, 1, pl.ds(x, 1), :] = p[0:1, :]
+        return 0
+
+    lax.fori_loop(0, 16, sweep, 0)
+    p2_x = x_pair(P2.at[16], P2.at[0], P2.at[1], P2.at[17], 4)
+    p2_y = y_pair(6)
+    for copy in p2_x + p2_y:
+        copy.start()
+
     finish(p2_x)
     finish(p2_y)
     clear_planes([(P2, P2.at[0], P2.at[17])])
@@ -351,24 +375,12 @@
 
     lax.fori_loop(0, 16, correct, 0)
 
-    def outs(k, lo, n):
-        return [
-            pltpu.make_async_copy(OV.at[:, pl.ds(lo, n)], vel_out.at[:, pl.ds(lo, n)], out_sem.at[2 * k]),
-            pltpu.make_async_copy(P2.at[pl.ds(lo + 1, n)], pres_out.at[pl.ds(lo, n)], out_sem.at[2 * k + 1]),
-        ]
-
-    early = outs(0, 4, 8)
-    late = outs(1, 0, 4) + outs(2, 12, 4)
-    for copy in early:
+    outs = [
+        pltpu.make_async_copy(OV, ov_out, out_sem.at[0]),
+        pltpu.make_async_copy(P2.at[pl.ds(1, 16)], p2_out, out_sem.at[1]),
+    ]
+    for copy in outs:
         copy.start()
-
-    loads[6].wait()
-    loads[7].wait()
-    ko = KO[...]
-    kc = KC[...]
-    rel = (ko & 7) * 32 + (kc >> 8) - (cross * 32 - 4)
-    RK[...] = jnp.where((rel >= 0) & (rel < 40), (ko >> 3) * 40 + rel, -1).astype(F32)
-    ZK[...] = (kc & 255).astype(F32)
 
     loads[5].wait()
     total = SB2[0]
@@ -379,36 +391,30 @@
         jnp.ones((8, 256), F32), total * total, (((1,), (1,)), ((), ())),
         precision=lax.Precision.HIGHEST, preferred_element_type=F32,
     )[0:1] * (1.0 / 256.0)
-    FB[...] = TG[...] * mean
-
-    def f1_copy(k):
-        return remote(FB, FA.at[cross, slab], f1s.at[k], f1r.at[slab], 7 + k, cross)
-
-    for k in range(2):
-        @pl.when(slab != 7 + k)
-        def _():
-            f1_copy(k).start()
+    FB[...] = TG[:, 0, 0, :] * mean
+
+    def f1_copy(s, d):
+        return remote(FB, FA.at[cross, slab], f1s.at[(s - 7) * 8 + d], f1r.at[0], s, cr(d))
+
+    def f1_sends(act):
+        for d in (4, 2, 6, 3, 5, 1, 7, 0):
+            for s in (7, 8):
+                if d:
+                    act(f1_copy(s, d))
+                else:
+                    @pl.when(slab != s)
+                    def _():
+                        act(f1_copy(s, 0))
+
+    f1_sends(lambda copy: copy.start())
 
     @pl.when((slab == 7) | (slab == 8))
     def _():
-        FA[cross, slab] = FB[...]
-        for s in range(16):
-            @pl.when(slab != s)
-            def _():
-                remote(FB, FA.at[cross, s], f1s.at[0], f1r.at[s], slab, cross).wait_recv()
-
-        f2 = [remote(FA.at[cross], FA.at[cross], f2s.at[d], f2r.at[d], slab, cr(d)) for d in range(1, 8)]
-        for copy in f2:
-            copy.start()
-
-        for d in range(1, 8):
-            src = FA.at[cr(8 - d)]
-            remote(src, src, f2s.at[d], f2r.at[d], slab, cross).wait_recv()
+        pltpu.make_async_copy(FB, FA.at[cross, slab], f1r.at[0]).start()
+        remote(FA, FA, f1s.at[0], f1r.at[0], slab, cross).wait_recv()
 
         r_of = (lax.broadcasted_iota(jnp.int32, (5, 16, 128), 0) * 16
                 + lax.broadcasted_iota(jnp.int32, (5, 16, 128), 1)).astype(F32).astype(BF16)
-        z_at = (lax.broadcasted_iota(jnp.int32, (16, 16, 128), 0) * 16
-                + lax.broadcasted_iota(jnp.int32, (16, 16, 128), 1)).astype(F32).astype(BF16)
         ACC[...] = jnp.zeros(ACC.shape, F32)
 
         def add(c, _):
@@ -416,7 +422,6 @@
                 q = c * 16 + s
                 lanes = pl.ds(s * 128, 128)
                 rk = jnp.broadcast_to(RK[pl.ds(q, 1), :], (16, 128)).astype(BF16)[None]
-                zk = jnp.broadcast_to(ZK[pl.ds(q, 1), :], (16, 128)).astype(BF16)[None]
                 f = FA[c, s]
                 hi = f.astype(BF16).astype(F32)
                 lo = f - hi
@@ -425,95 +430,22 @@
                     for n, part in enumerate((hi, lo)):
                         value = jnp.broadcast_to(part[i:i + 1], (16, 128)).astype(BF16)[None]
                         LHS[pl.ds((i * 2 + n) * 5, 5), :, lanes] = jnp.where(mask, value, jnp.zeros((5, 16, 128), BF16))
-                RHS[:, :, lanes] = jnp.where(z_at == zk, jnp.ones((1, 16, 128), BF16), jnp.zeros((16, 16, 128), BF16))
             ACC[...] += lax.dot_general(
-                LHS[...].reshape(480, 2048), RHS[...].reshape(256, 2048), (((1,), (1,)), ((), ())),
+                LHS[...].reshape(480, 2048), RHS[c].reshape(256, 2048), (((1,), (1,)), ((), ())),
                 preferred_element_type=F32,
             )
             return 0
 
         lax.fori_loop(0, 8, add, 0)
 
-        push = {}
         for i in range(3):
             for p in range(2):
                 at = i * 160 + p * 40
-                push[i, 127 + p] = 0.5 * (ACC[at:at + 40, :] + ACC[at + 80:at + 120, :])
-        row = lax.broadcasted_iota(jnp.int32, (40, 256), 0) + (cross * 32 - 4)
-        inside = (row >= 0) & (row < 256)
-
-        def within(a):
-            return jnp.where(inside, a, 0.0)
-
-        def ny(a):
-            return pltpu.roll(a, 39, 0)
-
-        def py(a):
-            return pltpu.roll(a, 1, 0)
-
-        div = {126: 0.5 * push[0, 127], 129: -0.5 * push[0, 128]}
-        for x, side in ((127, push[0, 128]), (128, -push[0, 127])):
-            a, b = push[1, x], push[2, x]
-            div[x] = within(0.5 * (side + (ny(a) - py(a)) + (z_next(b) - z_prev(b))))
-        one = {x: -SIXTH * div[x] for x in div}
-        two = {}
-        for x in range(125, 131):
-            s = None
-            if x in one:
-                a = one[x]
-                s = ny(a) + py(a) + z_next(a) + z_prev(a) - div[x]
-            for near in (x - 1, x + 1):
-                if near in one:
-                    s = one[near] if s is None else s + one[near]
-            two[x] = within(s * SIXTH)
-
-        def centre(a):
-            return pltpu.roll(a, 36, 0)[0:32]
-
-        def apply(first, local):
-            for n in range(4):
-                x = first + n
-                g = None
-                if x + 1 in two:
-                    g = two[x + 1]
-                if x - 1 in two:
-                    g = -two[x - 1] if g is None else g - two[x - 1]
-                vx = -0.5 * g
-                if x in (127, 128):
-                    vx = vx + push[0, x]
-                OV[0, local + n] += centre(vx)
-                if x in two:
-                    a = two[x]
-                    P2[local + n + 1] += centre(a)
-                    vy = -0.5 * (ny(a) - py(a))
-                    vz = -0.5 * (z_next(a) - z_prev(a))
-                    if x in (127, 128):
-                        vy = vy + push[1, x]
-                        vz = vz + push[2, x]
-                    OV[1, local + n] += centre(vy)
-                    OV[2, local + n] += centre(vz)
-
-        for copy in p2_x:
-            copy.wait_send()
-
-        @pl.when(slab == 7)
-        def _():
-            apply(124, 12)
-
-        @pl.when(slab == 8)
-        def _():
-            apply(128, 0)
-
-        for copy in f2:
-            copy.wait_send()
-
-    for copy in late:
-        copy.start()
-
-    @pl.when(slab == 7)
-    def _():
-        for t in others:
-            a1_copy(t).wait_send()
+                PUSH[i, p] = 0.5 * (ACC[at:at + 40, :] + ACC[at + 80:at + 120, :])
+        push = pltpu.make_async_copy(PUSH, push_out, out_sem.at[2])
+        push.start()
+        push.wait()
+
     for d in range(8):
         if d:
             a2[d].wait_send()
@@ -522,59 +454,176 @@
             e2_copy(d).wait_send()
         a3_copy(d).wait_send()
         e1_copy(d).wait_send()
-    for pair in pairs + v_edges + [pr_x, pr_y, p1_x, p1_y, p2_y]:
+    for pair in pairs + v_edges + [pr_x, pr_y, p1_x, p1_y, p2_x, p2_y]:
         for copy in pair:
             copy.wait_send()
+    f1_sends(lambda copy: copy.wait_send())
+    for copy in outs:
+        copy.wait()
+
+
+def finish_kernel(ov, p2, push_in, vel_out, pres_out, WV, WP, PUSH, load_sem, out_sem):
+    slab = lax.axis_index("slab")
+    cross = lax.axis_index("cross")
+
+    def straight(k, lo, n):
+        return [
+            pltpu.make_async_copy(ov.at[:, pl.ds(lo, n)], vel_out.at[:, pl.ds(lo, n)], out_sem.at[2 * k]),
+            pltpu.make_async_copy(p2.at[pl.ds(lo, n)], pres_out.at[pl.ds(lo, n)], out_sem.at[2 * k + 1]),
+        ]
+
+    def run(first, lo):
+        if first is not None:
+            loads = [
+                pltpu.make_async_copy(push_in, PUSH, load_sem.at[0]),
+                pltpu.make_async_copy(ov.at[:, pl.ds(lo, 4)], WV, load_sem.at[1]),
+                pltpu.make_async_copy(p2.at[pl.ds(lo, 4)], WP, load_sem.at[2]),
+            ]
+            for load in loads:
+                load.start()
+        if first is None:
+            copies = straight(0, 0, 16)
+        else:
+            copies = straight(0, 4 - lo // 3, 12)
+        for copy in copies:
+            copy.start()
+        if first is not None:
+            for load in loads:
+                load.wait()
+            correct(first, cross, PUSH, WV, WP)
+            late = [
+                pltpu.make_async_copy(WV, vel_out.at[:, pl.ds(lo, 4)], out_sem.at[2]),
+                pltpu.make_async_copy(WP, pres_out.at[pl.ds(lo, 4)], out_sem.at[3]),
+            ]
+            for copy in late:
+                copy.start()
+            copies = copies + late
+        for copy in copies:
+            copy.wait()
+
+    @pl.when(slab == 7)
+    def _():
+        run(124, 12)
+
+    @pl.when(slab == 8)
+    def _():
+        run(128, 0)
 
     @pl.when((slab != 7) & (slab != 8))
     def _():
-        for copy in p2_x:
-            copy.wait_send()
-    for k in range(2):
-        @pl.when(slab != 7 + k)
-        def _():
-            f1_copy(k).wait_send()
-    for copy in early + late:
-        copy.wait()
+        run(None, 0)
+
+
+def correct(first, cross, PUSH, WV, WP):
+    push = {(i, 127 + p): PUSH[i, p] for i in range(3) for p in range(2)}
+    row = lax.broadcasted_iota(jnp.int32, (40, 256), 0) + (cross * 32 - 4)
+    inside = (row >= 0) & (row < 256)
+
+    def within(a):
+        return jnp.where(inside, a, 0.0)
+
+    def ny(a):
+        return pltpu.roll(a, 39, 0)
+
+    def py(a):
+        return pltpu.roll(a, 1, 0)
+
+    div = {126: 0.5 * push[0, 127], 129: -0.5 * push[0, 128]}
+    for x, side in ((127, push[0, 128]), (128, -push[0, 127])):
+        a, b = push[1, x], push[2, x]
+        div[x] = within(0.5 * (side + (ny(a) - py(a)) + (z_next(b) - z_prev(b))))
+    one = {x: -SIXTH * div[x] for x in div}
+    two = {}
+    for x in range(125, 131):
+        s = None
+        if x in one:
+            a = one[x]
+            s = ny(a) + py(a) + z_next(a) + z_prev(a) - div[x]
+        for near in (x - 1, x + 1):
+            if near in one:
+                s = one[near] if s is None else s + one[near]
+        two[x] = within(s * SIXTH)
+
+    def centre(a):
+        return pltpu.roll(a, 36, 0)[0:32]
+
+    def apply(first):
+        for n in range(4):
+            x = first + n
+            g = None
+            if x + 1 in two:
+                g = two[x + 1]
+            if x - 1 in two:
+                g = -two[x - 1] if g is None else g - two[x - 1]
+            vx = -0.5 * g
+            if x in (127, 128):
+                vx = vx + push[0, x]
+            WV[0, n] += centre(vx)
+            if x in two:
+                a = two[x]
+                WP[n] += centre(a)
+                vy = -0.5 * (ny(a) - py(a))
+                vz = -0.5 * (z_next(a) - z_prev(a))
+                if x in (127, 128):
+                    vy = vy + push[1, x]
+                    vz = vz + push[2, x]
+                WV[1, n] += centre(vy)
+                WV[2, n] += centre(vz)
+
+    apply(first)
 
 
 def body(velocity, pressure, inv_influence, normals, sample_cells, tangents, force_owner, force_cell):
     any_space = pl.BlockSpec(memory_space=pl.ANY)
     dma = pltpu.SemaphoreType.DMA
     vm = pltpu.VMEM
-    return pl.pallas_call(
+    ov, p2, push = pl.pallas_call(
         kernel,
         out_shape=(
             jax.ShapeDtypeStruct(velocity.shape, F32),
             jax.ShapeDtypeStruct(pressure.shape, F32),
+            jax.ShapeDtypeStruct((3, 2, 40, 256), F32),
         ),
         in_specs=[any_space] * 8,
-        out_specs=(any_space, any_space),
+        out_specs=(any_space,) * 3,
         scratch_shapes=[
             vm((3, 18, 32, 256), F32), vm((18, 32, 256), F32), vm((3, 18, 32, 256), F32),
             vm((18, 32, 256), F32), vm((18, 32, 256), F32), vm((16, 32, 256), F32), vm((3, 16, 32, 256), F32),
             vm((7, 2, 16, 256), F32), vm((7, 2, 16, 256), F32),
             vm((3, 256, 256), F32), vm((384, 512), BF16), vm((8, 2, 128, 1024), BF16), vm((128, 256), jnp.int32),
             vm((128, 256), F32), vm((128, 256), F32), vm((128, 256), jnp.int32),
-            pltpu.SMEM((3, 128), F32), vm((3, 128), F32),
+            pltpu.SMEM((3, 128), F32), vm((3, 1, 1, 128), F32),
             vm((128, 128), jnp.int32), vm((128, 128), jnp.int32), vm((128, 128), F32), vm((128, 128), F32),
             vm((128, 256), F32), vm((8, 128, 256), F32), vm((8, 128, 256), BF16),
             vm((8, 128, 256), F32), vm((8, 128, 256), F32), vm((8, 128, 256), F32), vm((8, 128, 256), F32),
             vm((3, 128), F32), vm((8, 16, 3, 128), F32),
-            vm((30, 16, 2048), BF16), vm((16, 16, 2048), BF16), vm((480, 256), F32),
+            vm((30, 16, 2048), BF16), vm((8, 16, 16, 2048), BF16), vm((480, 256), F32), vm((3, 2, 40, 256), F32),
             dma((8,)), dma((1,)), dma((16,)), dma((1,)), dma((8,)), dma((8,)), dma((8,)), dma((8,)),
             dma((8, CHUNKS)), dma((8, CHUNKS)), dma((8,)), dma((8,)), dma((8,)), dma((8,)),
-            dma((2,)), dma((16,)), dma((8,)), dma((8,)), dma((5, 2)), dma((5, 2)), dma((7, 2)), dma((7, 2)),
-            dma((6,)),
+            dma((16,)), dma((1,)), dma((5, 2)), dma((5, 2)), dma((7, 2)), dma((7, 2)),
+            dma((3,)),
         ],
         compiler_params=pltpu.CompilerParams(
             collective_id=0, has_side_effects=True, vmem_limit_bytes=56 * 1024 * 1024
         ),
     )(
         velocity, pressure, inv_influence.reshape(8, 2, 128, 1024),
-        normals.reshape(3, 8, 128).transpose(1, 0, 2), sample_cells, tangents.reshape(3, 128),
+        normals.reshape(3, 8, 128).transpose(1, 0, 2), sample_cells, tangents,
         force_owner.reshape(128, 128), force_cell.reshape(128, 128),
     )
+    return pl.pallas_call(
+        finish_kernel,
+        out_shape=(
+            jax.ShapeDtypeStruct(velocity.shape, F32),
+            jax.ShapeDtypeStruct(pressure.shape, F32),
+        ),
+        in_specs=[any_space] * 3,
+        out_specs=(any_space,) * 2,
+        scratch_shapes=[
+            vm((3, 4, 32, 256), F32), vm((4, 32, 256), F32), vm((3, 2, 40, 256), F32), dma((3,)), dma((4,)),
+        ],
+        compiler_params=pltpu.CompilerParams(vmem_limit_bytes=16 * 1024 * 1024),
+    )(ov, p2, push)
 
 
 def solution(mesh):

time: 94.7 us -> 85.3 us (0.901)
  Pallas kernels: 88.7 us -> 81.1 us
  local copies, waits for them, and re-layouts: 4.84 us -> 3.39 us
    pallas_call x1, Pallas kernels: 88.7 us -> 79.2 us  [body(): pl.pallas_call(kernel, out_shape=(jax.ShapeDtypeStruct(velocity.shape, F3...]
    pallas_call x0 -> x1, Pallas kernels: none -> 1.87 us  [body(): pl.pallas_call(finish_kernel, out_shape=(jax.ShapeDtypeStruct(velocity.sh...]
    unnamed x5 -> x6, local copies, waits for them, and re-layouts: 4.84 us -> 3.39 us
where the time goes in v2:
time: 85.3 us; the launch traced here: 85.1 us
  Pallas kernels  81.1 us (95%)
  local copies, waits for them, and re-layouts  3.39 us (4%)
    pallas_call x1, Pallas kernels, body(): pl.pallas_call(kernel, out_shape=(jax.ShapeDtypeStruct(velocity.shape, F3...  79.2 us
    unnamed x6, local copies, waits for them, and re-layouts  3.39 us
    pallas_call x1, Pallas kernels, body(): pl.pallas_call(finish_kernel, out_shape=(jax.ShapeDtypeStruct(velocity.sh...  1.87 us

profile of v2, /device:TPU:6, one launch (start us, length us, event | category | flops | bytes accessed | tf_op | source)
XLA Modules:
  0.0 85.1 jit_solution(7479874517984063608)
XLA Ops:
  0.6 79.2 %shard_map.95 = (f32[3,16,32,256]{3,2,1,0:T(8,128)}, f32[16,32,256]{2,1,0:T(8,128)}, f32[3,2,40,256]{3,2,1,0:T(8,128)}) custom-call(f32[3,16,32,256]{3,2,1,0:T(8,128)} %vel.1, f32[16,32,256]{2,1,0:T(8,128)} %pres.1, bf16[8,2,128,1024]{3,2,1,0:T(8,128)(2,1)} %bitcast.6, f32[8,3,128]{2,1,0:T(4,128)} %bitcast.9, s32[1024,256]{1,0:T(8,128)} %cells.1, ...), custom_call_target="tpu_custom_call" | custom-call | tf_op jit(solution)/shard_map/pallas_call | solution.py:580
  79.8 0.0 copy-start
  79.9 1.4 %copy-done = f32[3,16,32,256]{3,2,1,0:T(8,128)S(1)} copy-done((f32[3,16,32,256]{3,2,1,0:T(8,128)S(1)}, f32[3,16,32,256]{3,2,1,0:T(8,128)}, u32[]{:S(2)}) %copy-start) | copy-done | bytes 1572888
  81.3 0.0 copy-start.1
  81.3 1.0 %copy-done.1 = f32[16,32,256]{2,1,0:T(8,128)S(1)} copy-done((f32[16,32,256]{2,1,0:T(8,128)S(1)}, f32[16,32,256]{2,1,0:T(8,128)}, u32[]{:S(2)}) %copy-start.1) | copy-done | bytes 524312
  82.3 0.0 copy-start.2
  82.3 0.9 %copy-done.2 = f32[3,2,40,256]{3,2,1,0:T(8,128)S(1)} copy-done((f32[3,2,40,256]{3,2,1,0:T(8,128)S(1)}, f32[3,2,40,256]{3,2,1,0:T(8,128)}, u32[]{:S(2)}) %copy-start.2) | copy-done | bytes 245784
  83.2 1.9 %shard_map.96 = (f32[3,16,32,256]{3,2,1,0:T(8,128)}, f32[16,32,256]{2,1,0:T(8,128)}) custom-call(f32[3,16,32,256]{3,2,1,0:T(8,128)S(1)} %copy-done, f32[16,32,256]{2,1,0:T(8,128)S(1)} %copy-done.1, f32[3,2,40,256]{3,2,1,0:T(8,128)S(1)} %copy-done.2), custom_call_target="tpu_custom_call" | custom-call | tf_op jit(solution)/shard_map/pallas_call | solution.py:614
Async XLA Ops:
  79.8 1.4 %copy-start = (f32[3,16,32,256]{3,2,1,0:T(8,128)S(1)}, f32[3,16,32,256]{3,2,1,0:T(8,128)}, u32[]{:S(2)}) copy-start(f32[3,16,32,256]{3,2,1,0:T(8,128)} %get-tuple-element.5.ov) | copy-start | bytes 4718596
  81.3 1.0 %copy-start.1 = (f32[16,32,256]{2,1,0:T(8,128)S(1)}, f32[16,32,256]{2,1,0:T(8,128)}, u32[]{:S(2)}) copy-start(f32[16,32,256]{2,1,0:T(8,128)} %get-tuple-element.6.p2) | copy-start | bytes 1572868
  82.3 0.9 %copy-start.2 = (f32[3,2,40,256]{3,2,1,0:T(8,128)S(1)}, f32[3,2,40,256]{3,2,1,0:T(8,128)}, u32[]{:S(2)}) copy-start(f32[3,2,40,256]{3,2,1,0:T(8,128)} %get-tuple-element.7.push_in) | copy-start | bytes 737284

commit v3 on v2

v3 whole, which is shorter than its diff:
```python
import functools

import jax
import jax.numpy as jnp
from jax import lax
from jax.experimental import pallas as pl
from jax.experimental.pallas import tpu as pltpu
from jax.sharding import PartitionSpec as P

MESH = pl.DeviceIdType.MESH
F32 = jnp.float32
BF16 = jnp.bfloat16
SIXTH = 1.0 / 6.0
GROUP = 16


def z_next(a):
    lane = lax.broadcasted_iota(jnp.int32, a.shape, 1)
    return jnp.where(lane == 255, 0.0, pltpu.roll(a, 255, 1))


def z_prev(a):
    lane = lax.broadcasted_iota(jnp.int32, a.shape, 1)
    return jnp.where(lane == 0, 0.0, pltpu.roll(a, 1, 1))


def y_next(a, edge):
    n = a.shape[0]
    row = lax.broadcasted_iota(jnp.int32, a.shape, 0)
    return jnp.where(row == n - 1, edge, pltpu.roll(a, n - 1, 0))


def y_prev(a, edge):
    n = a.shape[0]
    row = lax.broadcasted_iota(jnp.int32, a.shape, 0)
    return jnp.where(row == 0, edge, pltpu.roll(a, 1, 0))


def kernel(
    vel, pres, inv, nrm, cells, tang, owner, cell,
    ov_out, p2_out, push_out,
    V, P0, PR, P1, P2, DV, OV,
    EDGE_S, EDGE_R,
    PL, T, A, CI, ZB, YH, YL, NS, TG, KO, KC, RK, ZK,
    NFS, NF, NFB, SB, RB1, RB2, FB, FA, LHS, RHS, ACC, PUSH, PUSH2,
    load_sem, ns_sem, a1s, a1r, a2s, a2r, a3s, a3r, ns, nr, e1s, e1r, e2s, e2r,
    f1s, f1r, f2s, f2r, xs, xr, ys, yr, out_sem,
):
    slab = lax.axis_index("slab")
    cross = lax.axis_index("cross")
    h = lax.rem(slab, 2)
    chip = slab // 2
    sib = slab + 1 - 2 * h

    def remote(src, dst, ss, rs, s, c):
        return pltpu.make_async_remote_copy(
            src_ref=src, dst_ref=dst, send_sem=ss, recv_sem=rs, device_id=(s, c), device_id_type=MESH
        )

    def cr(d):
        return lax.rem(cross + d, 8)

    def sl(d):
        return lax.rem(slab + d, 16)

    loads = [
        pltpu.make_async_copy(vel, V.at[:, pl.ds(1, 16)], load_sem.at[0]),
        pltpu.make_async_copy(pres, P0.at[pl.ds(1, 16)], load_sem.at[1]),
        pltpu.make_async_copy(cells.at[pl.ds(pl.multiple_of(cross * 128, 128), 128)], CI, load_sem.at[2]),
        pltpu.make_async_copy(nrm.at[cross], NS, load_sem.at[3]),
        pltpu.make_async_copy(inv.at[:, 0], A.at[0], load_sem.at[4]),
        pltpu.make_async_copy(tang, TG, load_sem.at[5]),
        pltpu.make_async_copy(owner, KO, load_sem.at[6]),
        pltpu.make_async_copy(cell, KC, load_sem.at[7]),
        pltpu.make_async_copy(inv.at[:, 1], A.at[1], load_sem.at[8]),
    ]
    for n in (0, 1, 2, 3, 5, 6, 7):
        loads[n].start()

    barrier = pltpu.get_barrier_semaphore()
    for d in range(1, 16):
        pl.semaphore_signal(barrier, inc=1, device_id=(sl(d), cross), device_id_type=MESH)
    for d in range(1, 8):
        pl.semaphore_signal(barrier, inc=1, device_id=(slab, cr(d)), device_id_type=MESH)
    pl.semaphore_wait(barrier, 22)

    def a1_copy(target, k):
        half = target % 2
        return remote(
            vel.at[k, 8, pl.ds(half * 16, 16)],
            PL.at[k, pl.ds(pl.multiple_of(cross * 32 + half * 16, 16), 16)],
            a1s.at[k, target], a1r.at[k], target, cross,
        )

    def tile(c, half, k):
        return PL.at[k, pl.ds(pl.multiple_of(c * 32 + half * 16, 16), 16)]

    others = [t for t in (6, 8, 5, 4, 9, 2, 1, 3, 0, 10, 14, 15, 11, 13, 12)]

    @pl.when(slab == 7)
    def _():
        for k in range(3):
            pltpu.make_async_copy(vel.at[k, 8, pl.ds(16, 16)], tile(cross, 1, k), a1r.at[k]).start()
            for t in others:
                a1_copy(t, k).start()

    def x_pair(src_hi, dst_lo, src_lo, dst_hi, k):
        up = remote(src_hi, dst_lo, xs.at[k, 0], xr.at[k, 0], sl(1), cross)
        down = remote(src_lo, dst_hi, xs.at[k, 1], xr.at[k, 1], sl(15), cross)
        return up, down

    def y_pair(k):
        up = remote(EDGE_S.at[k, 0], EDGE_R.at[k, 0], ys.at[k, 0], yr.at[k, 0], slab, cr(1))
        down = remote(EDGE_S.at[k, 1], EDGE_R.at[k, 1], ys.at[k, 1], yr.at[k, 1], slab, cr(7))
        return up, down

    pairs = [x_pair(vel.at[:, 15], V.at[:, 0], vel.at[:, 0], V.at[:, 17], 0),
             x_pair(pres.at[15], P0.at[0], pres.at[0], P0.at[17], 1)]
    for pair in pairs:
        for copy in pair:
            copy.start()

    loads[0].wait()
    loads[1].wait()

    def fill_edges(k, source):
        def step(x, _):
            EDGE_S[k, 0, pl.ds(x, 1), :] = source(x, 31)
            EDGE_S[k, 1, pl.ds(x, 1), :] = source(x, 0)
            return 0
        lax.fori_loop(0, 16, step, 0)

    for i in range(3):
        fill_edges(i, lambda x, r, i=i: V[i, x + 1, r:r + 1, :])
    fill_edges(3, lambda x, r: P0[x + 1, r:r + 1, :])
    v_edges = [y_pair(k) for k in range(4)]
    for pair in v_edges:
        for copy in pair:
            copy.start()

    def finish(pair):
        for copy in pair:
            copy.wait_recv()

    def clear_planes(refs):
        @pl.when(slab == 0)
        def _():
            for ref, lo, hi in refs:
                lo[...] = jnp.zeros(lo.shape, F32)

        @pl.when(slab == 15)
        def _():
            for ref, lo, hi in refs:
                hi[...] = jnp.zeros(hi.shape, F32)

    def clear_rows(ks):
        @pl.when(cross == 0)
        def _():
            for k in ks:
                EDGE_R[k, 0] = jnp.zeros((16, 256), F32)

        @pl.when(cross == 7)
        def _():
            for k in ks:
                EDGE_R[k, 1] = jnp.zeros((16, 256), F32)

    loads[2].wait()
    for q in range(2):
        for n in range(2):
            ci = CI[n * 64:(n + 1) * 64, q * 128:(q + 1) * 128]
            side = slice(n * 128, (n + 1) * 128)
            ZB[q, :, side] = (ci & 255).astype(F32)
            YH[q, :, side] = (ci >> 15).astype(F32)
            YL[q, :, side] = (ci >> 8) & 127

    loads[6].wait()
    loads[7].wait()
    ko = KO[...]
    kc = KC[...]
    rel = (ko & 7) * 32 + (kc >> 8) - (cross * 32 - 4)
    RK[...] = jnp.where((rel >= 0) & (rel < 40), (ko >> 3) * 40 + rel, -1).astype(F32)
    ZK[...] = (kc & 255).astype(F32)

    def place_all():
        z_at = (lax.broadcasted_iota(jnp.int32, (16, 16, 128), 0) * 16
                + lax.broadcasted_iota(jnp.int32, (16, 16, 128), 1)).astype(F32).astype(BF16)

        def place(c, _):
            for s in range(16):
                zk = jnp.broadcast_to(ZK[pl.ds((h * 4 + c) * 16 + s, 1), :], (16, 128)).astype(BF16)[None]
                RHS[c, :, :, s * 128:(s + 1) * 128] = jnp.where(
                    z_at == zk, jnp.ones((1, 16, 128), BF16), jnp.zeros((16, 16, 128), BF16)
                )
            return 0
        lax.fori_loop(0, 4, place, 0)

    @pl.when((slab == 8) | (slab == 9))
    def _():
        place_all()

    def a2_copy(d, k):
        return remote(tile(cross, h, k), tile(cross, h, k), a2s.at[k, d], a2r.at[k, d], slab, cr(d))

    def a3_copy(d, k):
        src = tile(cr(8 - d), h, k)
        return remote(src, src, a3s.at[k, d], a3r.at[k, d], sib, cross)

    for k in range(3):
        remote(vel.at[k, 8, pl.ds(0, 16)], tile(cross, h, k), a1s.at[k, 0], a1r.at[k], slab, cross).wait_recv()
        for d in (4, 1, 7, 3, 5, 2, 6):
            a2_copy(d, k).start()
        a3_copy(0, k).start()

    loads[4].start()
    loads[8].start()

    @pl.when((slab == 6) | (slab == 7))
    def _():
        place_all()

    for pair in pairs:
        finish(pair)
    for pair in v_edges:
        finish(pair)
    clear_planes([(V, V.at[:, 0], V.at[:, 17]), (P0, P0.at[0], P0.at[17])])
    clear_rows(range(4))

    def around(u, lo, hi, k, x):
        mid = u(x + 1)
        s = u(x + 2) + u(x)
        s = s + y_next(mid, EDGE_R[k, 1, pl.ds(x, 1), :]) + y_prev(mid, EDGE_R[k, 0, pl.ds(x, 1), :])
        return s + z_next(mid) + z_prev(mid)

    def predict(x, _):
        for i in range(3):
            mid = V[i, x + 1]
            s = around(lambda q: V[i, q], None, None, i, x)
            pr = mid + 0.5 * (0.1 * (s - 6.0 * mid))
            PR[i, x + 1] = pr
            if i == 1:
                EDGE_S[4, 0, pl.ds(x, 1), :] = pr[31:32, :]
                EDGE_S[4, 1, pl.ds(x, 1), :] = pr[0:1, :]
        return 0

    lax.fori_loop(0, 16, predict, 0)
    pr_x = x_pair(PR.at[0, 16], PR.at[0, 0], PR.at[0, 1], PR.at[0, 17], 2)
    pr_y = y_pair(4)
    for copy in pr_x + pr_y:
        copy.start()

    for k in range(3):
        for d in (1, 7, 4, 3, 5, 2, 6):
            remote(tile(cross, h, k), tile(cr(8 - d), h, k), a2s.at[k, d], a2r.at[k, d], slab, cross).wait_recv()
            a3_copy(d, k).start()

    for k in range(3):
        for d in (0, 1, 7, 4, 3, 5, 2, 6):
            remote(tile(cross, h, k), tile(cr(8 - d), 1 - h, k), a3s.at[k, d], a3r.at[k, d], sib, cross).wait_recv()
    for c in range(3):
        for k in range(2):
            T[pl.ds(c * 128, 128), pl.ds(k * 256, 256)] = PL[c, pl.ds(k * 128, 128), :].astype(BF16)

    loads[3].wait()

    row16 = lax.broadcasted_iota(jnp.int32, (16, 16, 256), 0) * 16 + lax.broadcasted_iota(jnp.int32, (16, 16, 256), 1)
    z_of = row16.astype(F32).astype(BF16)
    y_of = lax.broadcasted_iota(jnp.int32, (16, 8, 256), 0) * 8 + lax.broadcasted_iota(jnp.int32, (16, 8, 256), 1)

    def lookup(q, m):
        zb = jnp.broadcast_to(ZB[q, pl.ds(m, 1), :], (16, 256)).astype(BF16)[None]
        yh = jnp.broadcast_to(YH[q, pl.ds(m, 1), :], (16, 256)).astype(BF16)[None]
        mask = z_of == zb
        zero = jnp.zeros((16, 16, 256), BF16)
        one = jnp.ones((1, 16, 256), BF16)
        hot = jnp.concatenate(
            [jnp.where(mask, one - yh, zero).reshape(256, 256), jnp.where(mask, yh, zero).reshape(256, 256)], axis=0
        )
        r = jnp.dot(T[...], hot, preferred_element_type=F32).reshape(3, 16, 8, 256)
        ym = y_of == jnp.broadcast_to(YL[q, pl.ds(m, 1), :], (8, 256))[None]
        a = [jnp.sum(jnp.where(ym, r[i], 0.0), axis=0) for i in range(3)]
        for n in range(2):
            side = slice(n * 128, (n + 1) * 128)
            j = n * 64 + m
            acc = NS[0, j] * a[0][:, side] + NS[1, j] * a[1][:, side] + NS[2, j] * a[2][:, side]
            NFS[q, n, pl.ds(m, 1), :] = jnp.sum(acc, axis=0, keepdims=True).astype(BF16).astype(F32)

    def nf_copy(q, d, part):
        return remote(NFS.at[q, :, part], NF.at[q, cross, :, part], ns.at[q, d], nr.at[q, d], slab, cr(d))

    def nf_wait(q):
        NFB[q, cross] = NFS[q].reshape(128, 128).astype(BF16)

        def take(d, _):
            src = cr(8 - d)
            remote(NFS.at[q], NF.at[q, src], ns.at[q, d], nr.at[q, d], slab, cross).wait_recv()
            NFB[q, src] = NF[q, src].reshape(128, 128).astype(BF16)
            return 0
        lax.fori_loop(1, 8, take, 0)

    def at(d):
        return lax.rem(chip + d, 8)

    def e1_copy(q, d):
        return remote(SB.at[q, 0, at(d)], RB1.at[q, at(d)], e1s.at[q, d], e1r.at[q, d], sib, cross)

    def e2_copy(q, d):
        return remote(SB.at[q, 1, at(d)], RB2.at[q, d], e2s.at[q, d], e2r.at[q, d], at(d) * 2 + h, cross)

    def e1_start(q):
        def part(t, _):
            half = lax.rem(h + 1 + t, 2)
            out = jnp.dot(A[half].reshape(1024, 1024), NFB[q].reshape(1024, 128), preferred_element_type=F32)
            SB[q, t] = out.reshape(8, 128, 128)

            @pl.when(t == 0)
            def _():
                for d in (1, 2, 3, 4, 5, 6, 7, 0):
                    e1_copy(q, d).start()
            return 0
        lax.fori_loop(0, 2, part, 0)

    def e2_start(q):
        for d in (1, 2, 3, 4, 5, 6, 7, 0):
            e1_copy(q, d).wait_recv()
            SB[q, 1, at(d)] += RB1[q, at(d)]
            if d:
                e2_copy(q, d).start()

    p1_x = x_pair(P1.at[16], P1.at[0], P1.at[1], P1.at[17], 3)
    p1_y = y_pair(5)

    def diverge_all():
        finish(pr_x)
        finish(pr_y)
        clear_planes([(PR, PR.at[0, 0], PR.at[0, 17])])
        clear_rows([4])

        def diverge(x, _):
            py = PR[1, x + 1]
            pz = PR[2, x + 1]
            g = PR[0, x + 2] - PR[0, x]
            g = g + (y_next(py, EDGE_R[4, 1, pl.ds(x, 1), :]) - y_prev(py, EDGE_R[4, 0, pl.ds(x, 1), :]))
            g = 0.5 * (g + (z_next(pz) - z_prev(pz)))
            DV[x] = g
            p = (around(lambda q: P0[q], None, None, 3, x) - g) * SIXTH
            P1[x + 1] = p
            EDGE_S[5, 0, pl.ds(x, 1), :] = p[31:32, :]
            EDGE_S[5, 1, pl.ds(x, 1), :] = p[0:1, :]
            return 0

        lax.fori_loop(0, 16, diverge, 0)
        for copy in p1_x + p1_y:
            copy.start()

    loads[4].wait()
    loads[8].wait()

    def step(it, _):
        q = it // 4
        first = lax.rem(it, 4) * GROUP

        @pl.when(it < 8)
        def _():
            for g in range(GROUP):
                lookup(q, first + g)
            for d in (4, 1, 7, 3, 5, 2, 6):
                nf_copy(q, d, pl.ds(pl.multiple_of(first, GROUP), GROUP)).start()

        @pl.when(it == 8)
        def _():
            diverge_all()

        @pl.when((it == 6) | (it == 8))
        def _():
            late = (it - 6) // 2
            nf_wait(late)
            e1_start(late)

        @pl.when(it == 7)
        def _():
            e2_start(0)
        return 0

    lax.fori_loop(0, 9, step, 0)
    e2_start(1)

    finish(p1_x)
    finish(p1_y)
    clear_planes([(P1, P1.at[0], P1.at[17])])
    clear_rows([5])

    def sweep(x, _):
        p = (around(lambda q: P1[q], None, None, 5, x) - DV[x]) * SIXTH
        P2[x + 1] = p
        EDGE_S[6, 0, pl.ds(x, 1), :] = p[31:32, :]
        EDGE_S[6, 1, pl.ds(x, 1), :] = p[0:1, :]
        return 0

    lax.fori_loop(0, 16, sweep, 0)
    p2_x = x_pair(P2.at[16], P2.at[0], P2.at[1], P2.at[17], 4)
    p2_y = y_pair(6)
    for copy in p2_x + p2_y:
        copy.start()

    finish(p2_x)
    finish(p2_y)
    clear_planes([(P2, P2.at[0], P2.at[17])])
    clear_rows([6])

    def correct(x, _):
        mid = P2[x + 1]
        OV[0, x] = PR[0, x + 1] - 0.5 * (P2[x + 2] - P2[x])
        gy = y_next(mid, EDGE_R[6, 1, pl.ds(x, 1), :]) - y_prev(mid, EDGE_R[6, 0, pl.ds(x, 1), :])
        OV[1, x] = PR[1, x + 1] - 0.5 * gy
        OV[2, x] = PR[2, x + 1] - 0.5 * (z_next(mid) - z_prev(mid))
        return 0

    lax.fori_loop(0, 16, correct, 0)

    outs = [
        pltpu.make_async_copy(OV, ov_out, out_sem.at[0]),
        pltpu.make_async_copy(P2.at[pl.ds(1, 16)], p2_out, out_sem.at[1]),
    ]
    for copy in outs:
        copy.start()

    loads[5].wait()
    square = None
    for q in range(2):
        total = SB[q, 1, chip]
        for d in range(1, 8):
            e2_copy(q, d).wait_recv()
            total = total + RB2[q, d]
        square = total * total if square is None else square + total * total
    mean = lax.dot_general(
        jnp.ones((8, 128), F32), square, (((1,), (1,)), ((), ())),
        precision=lax.Precision.HIGHEST, preferred_element_type=F32,
    )[0:1] * (1.0 / 256.0)
    FB[...] = TG[:, 0, 0, :] * mean

    side = cross // 4
    slot = lax.rem(cross, 4)

    def f1_copy(n, d):
        return remote(FB, FA.at[slot, slab], f1s.at[n * 8 + d], f1r.at[0], 6 + 2 * n + side, cr(d))

    def f1_sends(act):
        for d in (4, 2, 6, 3, 5, 1, 7, 0):
            for n in range(2):
                if d:
                    act(f1_copy(n, d))
                else:
                    @pl.when(slab != 6 + 2 * n + side)
                    def _():
                        act(f1_copy(n, 0))

    f1_sends(lambda copy: copy.start())

    @pl.when((slab >= 6) & (slab <= 9))
    def _():
        @pl.when(side == h)
        def _():
            pltpu.make_async_copy(FB, FA.at[slot, slab], f1r.at[0]).start()

        remote(FA, FA, f1s.at[0], f1r.at[0], slab, cross).wait_recv()

        r_of = (lax.broadcasted_iota(jnp.int32, (5, 16, 128), 0) * 16
                + lax.broadcasted_iota(jnp.int32, (5, 16, 128), 1)).astype(F32).astype(BF16)
        ACC[...] = jnp.zeros(ACC.shape, F32)

        def add(c, _):
            for s in range(16):
                q = (h * 4 + c) * 16 + s
                lanes = pl.ds(s * 128, 128)
                rk = jnp.broadcast_to(RK[pl.ds(q, 1), :], (16, 128)).astype(BF16)[None]
                f = FA[c, s]
                hi = f.astype(BF16).astype(F32)
                lo = f - hi
                mask = r_of == rk
                for i in range(3):
                    for n, part in enumerate((hi, lo)):
                        value = jnp.broadcast_to(part[i:i + 1], (16, 128)).astype(BF16)[None]
                        LHS[pl.ds((i * 2 + n) * 5, 5), :, lanes] = jnp.where(mask, value, jnp.zeros((5, 16, 128), BF16))
            ACC[...] += lax.dot_general(
                LHS[...].reshape(480, 2048), RHS[c].reshape(256, 2048), (((1,), (1,)), ((), ())),
                preferred_element_type=F32,
            )
            return 0

        lax.fori_loop(0, 4, add, 0)

        for i in range(3):
            for p in range(2):
                at = i * 160 + p * 40
                PUSH[i, p] = 0.5 * (ACC[at:at + 40, :] + ACC[at + 80:at + 120, :])
        share = remote(PUSH, PUSH2, f2s.at[0], f2r.at[0], sib, cross)

        @pl.when((slab == 6) | (slab == 9))
        def _():
            share.start()
            share.wait_send()

        @pl.when((slab == 7) | (slab == 8))
        def _():
            share.wait_recv()
            PUSH[...] += PUSH2[...]
            push = pltpu.make_async_copy(PUSH, push_out, out_sem.at[2])
            push.start()
            push.wait()

    @pl.when(slab == 7)
    def _():
        for k in range(3):
            for t in others:
                a1_copy(t, k).wait_send()
    for d in range(8):
        for k in range(3):
            if d:
                a2_copy(d, k).wait_send()
            a3_copy(d, k).wait_send()
        for q in range(2):
            if d:
                remote(NFS.at[q], NF.at[q, cross], ns.at[q, d], nr.at[q, d], slab, cr(d)).wait_send()
                e2_copy(q, d).wait_send()
            e1_copy(q, d).wait_send()
    for pair in pairs + v_edges + [pr_x, pr_y, p1_x, p1_y, p2_x, p2_y]:
        for copy in pair:
            copy.wait_send()
    f1_sends(lambda copy: copy.wait_send())
    for copy in outs:
        copy.wait()


def finish_kernel(ov, p2, push_in, vel_out, pres_out, WV, WP, PUSH, load_sem, out_sem):
    slab = lax.axis_index("slab")
    cross = lax.axis_index("cross")

    def moves(k, into):
        part = pl.ds(4 * k, 4)
        if into:
            return [
                pltpu.make_async_copy(ov.at[:, part], WV.at[:, part], load_sem.at[k]),
                pltpu.make_async_copy(p2.at[part], WP.at[part], load_sem.at[4 + k]),
            ]
        return [
            pltpu.make_async_copy(WV.at[:, part], vel_out.at[:, part], out_sem.at[k]),
            pltpu.make_async_copy(WP.at[part], pres_out.at[part], out_sem.at[4 + k]),
        ]

    def run(first, last):
        if first is not None:
            load = pltpu.make_async_copy(push_in, PUSH, load_sem.at[8])
            load.start()
        order = [k for k in range(4) if k != last] + [last]
        for k in [last] + order[:3]:
            for copy in moves(k, True):
                copy.start()
        for k in order:
            for copy in moves(k, True):
                copy.wait()
            if k == last and first is not None:
                load.wait()
                correct(first, 4 * k, cross, PUSH, WV, WP)
            for copy in moves(k, False):
                copy.start()
        for k in range(4):
            for copy in moves(k, False):
                copy.wait()

    @pl.when(slab == 7)
    def _():
        run(124, 3)

    @pl.when(slab == 8)
    def _():
        run(128, 0)

    @pl.when((slab != 7) & (slab != 8))
    def _():
        run(None, 3)


def correct(first, at, cross, PUSH, WV, WP):
    push = {(i, 127 + p): PUSH[i, p] for i in range(3) for p in range(2)}
    row = lax.broadcasted_iota(jnp.int32, (40, 256), 0) + (cross * 32 - 4)
    inside = (row >= 0) & (row < 256)

    def within(a):
        return jnp.where(inside, a, 0.0)

    def ny(a):
        return pltpu.roll(a, 39, 0)

    def py(a):
        return pltpu.roll(a, 1, 0)

    div = {126: 0.5 * push[0, 127], 129: -0.5 * push[0, 128]}
    for x, side in ((127, push[0, 128]), (128, -push[0, 127])):
        a, b = push[1, x], push[2, x]
        div[x] = within(0.5 * (side + (ny(a) - py(a)) + (z_next(b) - z_prev(b))))
    one = {x: -SIXTH * div[x] for x in div}
    two = {}
    for x in range(125, 131):
        s = None
        if x in one:
            a = one[x]
            s = ny(a) + py(a) + z_next(a) + z_prev(a) - div[x]
        for near in (x - 1, x + 1):
            if near in one:
                s = one[near] if s is None else s + one[near]
        two[x] = within(s * SIXTH)

    def centre(a):
        return pltpu.roll(a, 36, 0)[0:32]

    def apply(first):
        for n in range(4):
            x = first + n
            g = None
            if x + 1 in two:
                g = two[x + 1]
            if x - 1 in two:
                g = -two[x - 1] if g is None else g - two[x - 1]
            vx = -0.5 * g
            if x in (127, 128):
                vx = vx + push[0, x]
            WV[0, at + n] += centre(vx)
            if x in two:
                a = two[x]
                WP[at + n] += centre(a)
                vy = -0.5 * (ny(a) - py(a))
                vz = -0.5 * (z_next(a) - z_prev(a))
                if x in (127, 128):
                    vy = vy + push[1, x]
                    vz = vz + push[2, x]
                WV[1, at + n] += centre(vy)
                WV[2, at + n] += centre(vz)

    apply(first)


def body(velocity, pressure, inv_influence, normals, sample_cells, tangents, force_owner, force_cell):
    any_space = pl.BlockSpec(memory_space=pl.ANY)
    dma = pltpu.SemaphoreType.DMA
    vm = pltpu.VMEM
    ov, p2, push = pl.pallas_call(
        kernel,
        out_shape=(
            jax.ShapeDtypeStruct(velocity.shape, F32),
            jax.ShapeDtypeStruct(pressure.shape, F32),
            jax.ShapeDtypeStruct((3, 2, 40, 256), F32),
        ),
        in_specs=[any_space] * 8,
        out_specs=(any_space,) * 3,
        scratch_shapes=[
            vm((3, 18, 32, 256), F32), vm((18, 32, 256), F32), vm((3, 18, 32, 256), F32),
            vm((18, 32, 256), F32), vm((18, 32, 256), F32), vm((16, 32, 256), F32), vm((3, 16, 32, 256), F32),
            vm((7, 2, 16, 256), F32), vm((7, 2, 16, 256), F32),
            vm((3, 256, 256), F32), vm((384, 512), BF16), vm((2, 8, 128, 1024), BF16), vm((128, 256), jnp.int32),
            vm((2, 64, 256), F32), vm((2, 64, 256), F32), vm((2, 64, 256), jnp.int32),
            pltpu.SMEM((3, 128), F32), vm((3, 1, 1, 128), F32),
            vm((128, 128), jnp.int32), vm((128, 128), jnp.int32), vm((128, 128), F32), vm((128, 128), F32),
            vm((2, 2, 64, 128), F32), vm((2, 8, 2, 64, 128), F32), vm((2, 8, 128, 128), BF16),
            vm((2, 2, 8, 128, 128), F32), vm((2, 8, 128, 128), F32), vm((2, 8, 128, 128), F32),
            vm((3, 128), F32), vm((4, 16, 3, 128), F32),
            vm((30, 16, 2048), BF16), vm((4, 16, 16, 2048), BF16), vm((480, 256), F32), vm((3, 2, 40, 256), F32), vm((3, 2, 40, 256), F32),
            dma((9,)), dma((1,)), dma((3, 16)), dma((3,)), dma((3, 8)), dma((3, 8)), dma((3, 8)), dma((3, 8)),
            dma((2, 8)), dma((2, 8)), dma((2, 8)), dma((2, 8)), dma((2, 8)), dma((2, 8)),
            dma((16,)), dma((1,)), dma((1,)), dma((1,)), dma((5, 2)), dma((5, 2)), dma((7, 2)), dma((7, 2)),
            dma((3,)),
        ],
        compiler_params=pltpu.CompilerParams(
            collective_id=0, has_side_effects=True, vmem_limit_bytes=56 * 1024 * 1024
        ),
    )(
        velocity, pressure, inv_influence.reshape(8, 2, 128, 1024),
        normals.reshape(3, 8, 128).transpose(1, 0, 2), sample_cells, tangents,
        force_owner.reshape(128, 128), force_cell.reshape(128, 128),
    )
    return pl.pallas_call(
        finish_kernel,
        out_shape=(
            jax.ShapeDtypeStruct(velocity.shape, F32),
            jax.ShapeDtypeStruct(pressure.shape, F32),
        ),
        in_specs=[any_space] * 3,
        out_specs=(any_space,) * 2,
        scratch_shapes=[
            vm((3, 16, 32, 256), F32), vm((16, 32, 256), F32), vm((3, 2, 40, 256), F32), dma((9,)), dma((8,)),
        ],
        compiler_params=pltpu.CompilerParams(vmem_limit_bytes=56 * 1024 * 1024),
    )(ov, p2, push)


def solution(mesh):
    return jax.shard_map(
        body,
        mesh=mesh,
        in_specs=(
            P(None, "slab", "cross", None),
            P("slab", "cross", None),
            P("cross", "slab"),
            P(None, "slab"),
            P("slab", None),
            P(None, "cross", "slab", None),
            P(),
            P(),
        ),
        out_specs=(P(None, "slab", "cross", None), P("slab", "cross", None)),
        check_vma=False,
    )
```

time: 85.3 us -> 76.9 us (0.902)
  Pallas kernels: 81.1 us -> 75.9 us
  local copies, waits for them, and re-layouts: 3.39 us -> 0 us
    pallas_call x1, Pallas kernels: 79.2 us -> 72.9 us  [body(): pl.pallas_call(kernel, out_shape=(jax.ShapeDtypeStruct(velocity.shape, F3...]
    unnamed x6 -> x0, local copies, waits for them, and re-layouts: 3.39 us -> none
    pallas_call x1, Pallas kernels: 1.87 us -> 2.98 us  [body(): pl.pallas_call(finish_kernel, out_shape=(jax.ShapeDtypeStruct(velocity.sh...]
where the time goes in v3:
time: 76.9 us; the launch traced here: 76.6 us
  Pallas kernels  75.9 us (99%)
    pallas_call x1, Pallas kernels, body(): pl.pallas_call(kernel, out_shape=(jax.ShapeDtypeStruct(velocity.shape, F3...  72.9 us
    pallas_call x1, Pallas kernels, body(): pl.pallas_call(finish_kernel, out_shape=(jax.ShapeDtypeStruct(velocity.sh...  2.98 us

profile of v3, /device:TPU:6, one launch (start us, length us, event | category | flops | bytes accessed | tf_op | source)
XLA Modules:
  0.0 76.6 jit_solution(7748909045885675365)
XLA Ops:
  0.6 72.9 %shard_map.95 = (f32[3,16,32,256]{3,2,1,0:T(8,128)}, f32[16,32,256]{2,1,0:T(8,128)}, f32[3,2,40,256]{3,2,1,0:T(8,128)}) custom-call(f32[3,16,32,256]{3,2,1,0:T(8,128)} %vel.1, f32[16,32,256]{2,1,0:T(8,128)} %pres.1, bf16[8,2,128,1024]{3,2,1,0:T(8,128)(2,1)} %bitcast.6, f32[8,3,128]{2,1,0:T(4,128)} %bitcast.9, s32[1024,256]{1,0:T(8,128)} %cells.1, ...), custom_call_target="tpu_custom_call" | custom-call | tf_op jit(solution)/shard_map/pallas_call | solution.py:646
  73.6 3.0 %shard_map.96 = (f32[3,16,32,256]{3,2,1,0:T(8,128)}, f32[16,32,256]{2,1,0:T(8,128)}) custom-call(f32[3,16,32,256]{3,2,1,0:T(8,128)} %get-tuple-element.5.ov, f32[16,32,256]{2,1,0:T(8,128)} %get-tuple-element.6.p2, f32[3,2,40,256]{3,2,1,0:T(8,128)} %get-tuple-element.7.push_in), custom_call_target="tpu_custom_call" | custom-call | tf_op jit(solution)/shard_map/pallas_call | solution.py:680

commit v4 on v3

--- a/solution.py
+++ b/solution.py
@@ -116,27 +116,12 @@
 
     pairs = [x_pair(vel.at[:, 15], V.at[:, 0], vel.at[:, 0], V.at[:, 17], 0),
              x_pair(pres.at[15], P0.at[0], pres.at[0], P0.at[17], 1)]
-    for pair in pairs:
-        for copy in pair:
-            copy.start()
-
-    loads[0].wait()
-    loads[1].wait()
-
     def fill_edges(k, source):
         def step(x, _):
             EDGE_S[k, 0, pl.ds(x, 1), :] = source(x, 31)
             EDGE_S[k, 1, pl.ds(x, 1), :] = source(x, 0)
             return 0
         lax.fori_loop(0, 16, step, 0)
-
-    for i in range(3):
-        fill_edges(i, lambda x, r, i=i: V[i, x + 1, r:r + 1, :])
-    fill_edges(3, lambda x, r: P0[x + 1, r:r + 1, :])
-    v_edges = [y_pair(k) for k in range(4)]
-    for pair in v_edges:
-        for copy in pair:
-            copy.start()
 
     def finish(pair):
         for copy in pair:
@@ -218,35 +203,18 @@
     def _():
         place_all()
 
+    loads[0].wait()
+    loads[1].wait()
+    for i in range(3):
+        fill_edges(i, lambda x, r, i=i: V[i, x + 1, r:r + 1, :])
+    fill_edges(3, lambda x, r: P0[x + 1, r:r + 1, :])
+    v_edges = [y_pair(k) for k in range(4)]
+    for pair in v_edges:
+        for copy in pair:
+            copy.start()
     for pair in pairs:
-        finish(pair)
-    for pair in v_edges:
-        finish(pair)
-    clear_planes([(V, V.at[:, 0], V.at[:, 17]), (P0, P0.at[0], P0.at[17])])
-    clear_rows(range(4))
-
-    def around(u, lo, hi, k, x):
-        mid = u(x + 1)
-        s = u(x + 2) + u(x)
-        s = s + y_next(mid, EDGE_R[k, 1, pl.ds(x, 1), :]) + y_prev(mid, EDGE_R[k, 0, pl.ds(x, 1), :])
-        return s + z_next(mid) + z_prev(mid)
-
-    def predict(x, _):
-        for i in range(3):
-            mid = V[i, x + 1]
-            s = around(lambda q: V[i, q], None, None, i, x)
-            pr = mid + 0.5 * (0.1 * (s - 6.0 * mid))
-            PR[i, x + 1] = pr
-            if i == 1:
-                EDGE_S[4, 0, pl.ds(x, 1), :] = pr[31:32, :]
-                EDGE_S[4, 1, pl.ds(x, 1), :] = pr[0:1, :]
-        return 0
-
-    lax.fori_loop(0, 16, predict, 0)
-    pr_x = x_pair(PR.at[0, 16], PR.at[0, 0], PR.at[0, 1], PR.at[0, 17], 2)
-    pr_y = y_pair(4)
-    for copy in pr_x + pr_y:
-        copy.start()
+        for copy in pair:
+            copy.start()
 
     for k in range(3):
         for d in (1, 7, 4, 3, 5, 2, 6):
@@ -314,17 +282,49 @@
 
             @pl.when(t == 0)
             def _():
-                for d in (1, 2, 3, 4, 5, 6, 7, 0):
+                for d in (6, 4, 2, 5, 7, 1, 3, 0):
                     e1_copy(q, d).start()
             return 0
         lax.fori_loop(0, 2, part, 0)
 
     def e2_start(q):
-        for d in (1, 2, 3, 4, 5, 6, 7, 0):
+        for d in (6, 4, 2, 5, 7, 1, 3, 0):
             e1_copy(q, d).wait_recv()
             SB[q, 1, at(d)] += RB1[q, at(d)]
             if d:
                 e2_copy(q, d).start()
+
+    def around(u, lo, hi, k, x):
+        mid = u(x + 1)
+        s = u(x + 2) + u(x)
+        s = s + y_next(mid, EDGE_R[k, 1, pl.ds(x, 1), :]) + y_prev(mid, EDGE_R[k, 0, pl.ds(x, 1), :])
+        return s + z_next(mid) + z_prev(mid)
+
+    def predict(x, _):
+        for i in range(3):
+            mid = V[i, x + 1]
+            s = around(lambda q: V[i, q], None, None, i, x)
+            pr = mid + 0.5 * (0.1 * (s - 6.0 * mid))
+            PR[i, x + 1] = pr
+            if i == 1:
+                EDGE_S[4, 0, pl.ds(x, 1), :] = pr[31:32, :]
+                EDGE_S[4, 1, pl.ds(x, 1), :] = pr[0:1, :]
+        return 0
+
+    pr_x = x_pair(PR.at[0, 16], PR.at[0, 0], PR.at[0, 1], PR.at[0, 17], 2)
+    pr_y = y_pair(4)
+
+    def predict_all():
+        for pair in pairs:
+            finish(pair)
+        for pair in v_edges:
+            finish(pair)
+        clear_planes([(V, V.at[:, 0], V.at[:, 17]), (P0, P0.at[0], P0.at[17])])
+        clear_rows(range(4))
+
+        lax.fori_loop(0, 16, predict, 0)
+        for copy in pr_x + pr_y:
+            copy.start()
 
     p1_x = x_pair(P1.at[16], P1.at[0], P1.at[1], P1.at[17], 3)
     p1_y = y_pair(5)
@@ -368,61 +368,20 @@
 
         @pl.when(it == 8)
         def _():
-            diverge_all()
-
-        @pl.when((it == 6) | (it == 8))
-        def _():
-            late = (it - 6) // 2
+            e2_start(0)
+            predict_all()
+
+        @pl.when((it == 7) | (it == 8))
+        def _():
+            late = it - 7
             nf_wait(late)
             e1_start(late)
 
-        @pl.when(it == 7)
-        def _():
-            e2_start(0)
         return 0
 
     lax.fori_loop(0, 9, step, 0)
     e2_start(1)
-
-    finish(p1_x)
-    finish(p1_y)
-    clear_planes([(P1, P1.at[0], P1.at[17])])
-    clear_rows([5])
-
-    def sweep(x, _):
-        p = (around(lambda q: P1[q], None, None, 5, x) - DV[x]) * SIXTH
-        P2[x + 1] = p
-        EDGE_S[6, 0, pl.ds(x, 1), :] = p[31:32, :]
-        EDGE_S[6, 1, pl.ds(x, 1), :] = p[0:1, :]
-        return 0
-
-    lax.fori_loop(0, 16, sweep, 0)
-    p2_x = x_pair(P2.at[16], P2.at[0], P2.at[1], P2.at[17], 4)
-    p2_y = y_pair(6)
-    for copy in p2_x + p2_y:
-        copy.start()
-
-    finish(p2_x)
-    finish(p2_y)
-    clear_planes([(P2, P2.at[0], P2.at[17])])
-    clear_rows([6])
-
-    def correct(x, _):
-        mid = P2[x + 1]
-        OV[0, x] = PR[0, x + 1] - 0.5 * (P2[x + 2] - P2[x])
-        gy = y_next(mid, EDGE_R[6, 1, pl.ds(x, 1), :]) - y_prev(mid, EDGE_R[6, 0, pl.ds(x, 1), :])
-        OV[1, x] = PR[1, x + 1] - 0.5 * gy
-        OV[2, x] = PR[2, x + 1] - 0.5 * (z_next(mid) - z_prev(mid))
-        return 0
-
-    lax.fori_loop(0, 16, correct, 0)
-
-    outs = [
-        pltpu.make_async_copy(OV, ov_out, out_sem.at[0]),
-        pltpu.make_async_copy(P2.at[pl.ds(1, 16)], p2_out, out_sem.at[1]),
-    ]
-    for copy in outs:
-        copy.start()
+    diverge_all()
 
     loads[5].wait()
     square = None
@@ -455,6 +414,46 @@
                         act(f1_copy(n, 0))
 
     f1_sends(lambda copy: copy.start())
+
+    finish(p1_x)
+    finish(p1_y)
+    clear_planes([(P1, P1.at[0], P1.at[17])])
+    clear_rows([5])
+
+    def sweep(x, _):
+        p = (around(lambda q: P1[q], None, None, 5, x) - DV[x]) * SIXTH
+        P2[x + 1] = p
+        EDGE_S[6, 0, pl.ds(x, 1), :] = p[31:32, :]
+        EDGE_S[6, 1, pl.ds(x, 1), :] = p[0:1, :]
+        return 0
+
+    lax.fori_loop(0, 16, sweep, 0)
+    p2_x = x_pair(P2.at[16], P2.at[0], P2.at[1], P2.at[17], 4)
+    p2_y = y_pair(6)
+    for copy in p2_x + p2_y:
+        copy.start()
+
+    finish(p2_x)
+    finish(p2_y)
+    clear_planes([(P2, P2.at[0], P2.at[17])])
+    clear_rows([6])
+
+    def correct(x, _):
+        mid = P2[x + 1]
+        OV[0, x] = PR[0, x + 1] - 0.5 * (P2[x + 2] - P2[x])
+        gy = y_next(mid, EDGE_R[6, 1, pl.ds(x, 1), :]) - y_prev(mid, EDGE_R[6, 0, pl.ds(x, 1), :])
+        OV[1, x] = PR[1, x + 1] - 0.5 * gy
+        OV[2, x] = PR[2, x + 1] - 0.5 * (z_next(mid) - z_prev(mid))
+        return 0
+
+    lax.fori_loop(0, 16, correct, 0)
+
+    outs = [
+        pltpu.make_async_copy(OV, ov_out, out_sem.at[0]),
+        pltpu.make_async_copy(P2.at[pl.ds(1, 16)], p2_out, out_sem.at[1]),
+    ]
+    for copy in outs:
+        copy.start()
 
     @pl.when((slab >= 6) & (slab <= 9))
     def _():

time: 76.9 us -> 73.5 us (0.956)
  Pallas kernels: 75.9 us -> 71.8 us
    pallas_call x1, Pallas kernels: 72.9 us -> 68.8 us  [body(): pl.pallas_call(kernel, out_shape=(jax.ShapeDtypeStruct(velocity.shape, F3...]
where the time goes in v4:
time: 73.5 us; the launch traced here: 72.4 us
  Pallas kernels  71.8 us (98%)
    pallas_call x1, Pallas kernels, body(): pl.pallas_call(kernel, out_shape=(jax.ShapeDtypeStruct(velocity.shape, F3...  68.8 us
    pallas_call x1, Pallas kernels, body(): pl.pallas_call(finish_kernel, out_shape=(jax.ShapeDtypeStruct(velocity.sh...  2.98 us

profile of v4, /device:TPU:6, one launch (start us, length us, event | category | flops | bytes accessed | tf_op | source)
XLA Modules:
  0.0 72.4 jit_solution(14129835629241478478)
XLA Ops:
  0.6 68.8 %shard_map.95 = (f32[3,16,32,256]{3,2,1,0:T(8,128)}, f32[16,32,256]{2,1,0:T(8,128)}, f32[3,2,40,256]{3,2,1,0:T(8,128)}) custom-call(f32[3,16,32,256]{3,2,1,0:T(8,128)} %vel.1, f32[16,32,256]{2,1,0:T(8,128)} %pres.1, bf16[8,2,128,1024]{3,2,1,0:T(8,128)(2,1)} %bitcast.6, f32[8,3,128]{2,1,0:T(4,128)} %bitcast.9, s32[1024,256]{1,0:T(8,128)} %cells.1, ...), custom_call_target="tpu_custom_call" | custom-call | tf_op jit(solution)/shard_map/pallas_call | solution.py:645
  69.4 3.0 %shard_map.96 = (f32[3,16,32,256]{3,2,1,0:T(8,128)}, f32[16,32,256]{2,1,0:T(8,128)}) custom-call(f32[3,16,32,256]{3,2,1,0:T(8,128)} %get-tuple-element.5.ov, f32[16,32,256]{2,1,0:T(8,128)} %get-tuple-element.6.p2, f32[3,2,40,256]{3,2,1,0:T(8,128)} %get-tuple-element.7.push_in), custom_call_target="tpu_custom_call" | custom-call | tf_op jit(solution)/shard_map/pallas_call | solution.py:679

commit v5 on v4

--- a/solution.py
+++ b/solution.py
@@ -11,7 +11,8 @@
 F32 = jnp.float32
 BF16 = jnp.bfloat16
 SIXTH = 1.0 / 6.0
-GROUP = 16
+GROUP = 32
+PARTS = 64 // GROUP
 
 
 def z_next(a):
@@ -60,6 +61,12 @@
     def cr(d):
         return lax.rem(cross + d, 8)
 
+    def peer(d):
+        return lax.rem(cross // 4 + d // 4, 2) * 4 + lax.rem(cross + d, 4)
+
+    def peer_in(d):
+        return lax.rem(cross // 4 + d // 4, 2) * 4 + lax.rem(cross + 8 - d, 4)
+
     def sl(d):
         return lax.rem(slab + d, 16)
 
@@ -184,15 +191,15 @@
         place_all()
 
     def a2_copy(d, k):
-        return remote(tile(cross, h, k), tile(cross, h, k), a2s.at[k, d], a2r.at[k, d], slab, cr(d))
+        return remote(tile(cross, h, k), tile(cross, h, k), a2s.at[k, d], a2r.at[k, d], slab, peer(d))
 
     def a3_copy(d, k):
-        src = tile(cr(8 - d), h, k)
+        src = tile(peer_in(d), h, k)
         return remote(src, src, a3s.at[k, d], a3r.at[k, d], sib, cross)
 
     for k in range(3):
         remote(vel.at[k, 8, pl.ds(0, 16)], tile(cross, h, k), a1s.at[k, 0], a1r.at[k], slab, cross).wait_recv()
-        for d in (4, 1, 7, 3, 5, 2, 6):
+        for d in (6, 5, 7, 4, 2, 1, 3):
             a2_copy(d, k).start()
         a3_copy(0, k).start()
 
@@ -218,12 +225,12 @@
 
     for k in range(3):
         for d in (1, 7, 4, 3, 5, 2, 6):
-            remote(tile(cross, h, k), tile(cr(8 - d), h, k), a2s.at[k, d], a2r.at[k, d], slab, cross).wait_recv()
+            remote(tile(cross, h, k), tile(peer_in(d), h, k), a2s.at[k, d], a2r.at[k, d], slab, cross).wait_recv()
             a3_copy(d, k).start()
 
     for k in range(3):
         for d in (0, 1, 7, 4, 3, 5, 2, 6):
-            remote(tile(cross, h, k), tile(cr(8 - d), 1 - h, k), a3s.at[k, d], a3r.at[k, d], sib, cross).wait_recv()
+            remote(tile(cross, h, k), tile(peer_in(d), 1 - h, k), a3s.at[k, d], a3r.at[k, d], sib, cross).wait_recv()
     for c in range(3):
         for k in range(2):
             T[pl.ds(c * 128, 128), pl.ds(k * 256, 256)] = PL[c, pl.ds(k * 128, 128), :].astype(BF16)
@@ -253,20 +260,20 @@
             NFS[q, n, pl.ds(m, 1), :] = jnp.sum(acc, axis=0, keepdims=True).astype(BF16).astype(F32)
 
     def nf_copy(q, d, part):
-        return remote(NFS.at[q, :, part], NF.at[q, cross, :, part], ns.at[q, d], nr.at[q, d], slab, cr(d))
+        return remote(NFS.at[q, :, part], NF.at[q, cross, :, part], ns.at[q, d], nr.at[q, d], slab, peer(d))
 
     def nf_wait(q):
         NFB[q, cross] = NFS[q].reshape(128, 128).astype(BF16)
 
         def take(d, _):
-            src = cr(8 - d)
+            src = peer_in(d)
             remote(NFS.at[q], NF.at[q, src], ns.at[q, d], nr.at[q, d], slab, cross).wait_recv()
             NFB[q, src] = NF[q, src].reshape(128, 128).astype(BF16)
             return 0
         lax.fori_loop(1, 8, take, 0)
 
     def at(d):
-        return lax.rem(chip + d, 8)
+        return lax.rem(chip // 4 + d // 4, 2) * 4 + lax.rem(chip + d, 4)
 
     def e1_copy(q, d):
         return remote(SB.at[q, 0, at(d)], RB1.at[q, at(d)], e1s.at[q, d], e1r.at[q, d], sib, cross)
@@ -282,13 +289,13 @@
 
             @pl.when(t == 0)
             def _():
-                for d in (6, 4, 2, 5, 7, 1, 3, 0):
+                for d in (6, 5, 7, 4, 2, 1, 3, 0):
                     e1_copy(q, d).start()
             return 0
         lax.fori_loop(0, 2, part, 0)
 
     def e2_start(q):
-        for d in (6, 4, 2, 5, 7, 1, 3, 0):
+        for d in (6, 5, 7, 4, 2, 1, 3, 0):
             e1_copy(q, d).wait_recv()
             SB[q, 1, at(d)] += RB1[q, at(d)]
             if d:
@@ -356,32 +363,50 @@
     loads[8].wait()
 
     def step(it, _):
-        q = it // 4
-        first = lax.rem(it, 4) * GROUP
-
-        @pl.when(it < 8)
+        q = it // PARTS
+        first = lax.rem(it, PARTS) * GROUP
+
+        @pl.when(it < 2 * PARTS)
         def _():
             for g in range(GROUP):
                 lookup(q, first + g)
-            for d in (4, 1, 7, 3, 5, 2, 6):
+            for d in (6, 5, 7, 4, 2, 1, 3):
                 nf_copy(q, d, pl.ds(pl.multiple_of(first, GROUP), GROUP)).start()
 
-        @pl.when(it == 8)
+        @pl.when(it == 2 * PARTS)
         def _():
             e2_start(0)
             predict_all()
 
-        @pl.when((it == 7) | (it == 8))
-        def _():
-            late = it - 7
+        @pl.when(it >= 2 * PARTS - 1)
+        def _():
+            late = it - (2 * PARTS - 1)
             nf_wait(late)
             e1_start(late)
 
         return 0
 
-    lax.fori_loop(0, 9, step, 0)
+    lax.fori_loop(0, 2 * PARTS + 1, step, 0)
     e2_start(1)
     diverge_all()
+
+    @pl.when(slab == 7)
+    def _():
+        for k in range(3):
+            for t in others:
+                a1_copy(t, k).wait_send()
+    for d in range(8):
+        for k in range(3):
+            if d:
+                a2_copy(d, k).wait_send()
+            a3_copy(d, k).wait_send()
+        for q in range(2):
+            if d:
+                remote(NFS.at[q], NF.at[q, cross], ns.at[q, d], nr.at[q, d], slab, peer(d)).wait_send()
+            e1_copy(q, d).wait_send()
+    for pair in pairs + v_edges + [pr_x, pr_y]:
+        for copy in pair:
+            copy.wait_send()
 
     loads[5].wait()
     square = None
@@ -414,6 +439,12 @@
                         act(f1_copy(n, 0))
 
     f1_sends(lambda copy: copy.start())
+
+    for q in range(2):
+        for d in range(1, 8):
+            e2_copy(q, d).wait_send()
+    for copy in p1_x + p1_y:
+        copy.wait_send()
 
     finish(p1_x)
     finish(p1_y)
@@ -507,24 +538,8 @@
             push.start()
             push.wait()
 
-    @pl.when(slab == 7)
-    def _():
-        for k in range(3):
-            for t in others:
-                a1_copy(t, k).wait_send()
-    for d in range(8):
-        for k in range(3):
-            if d:
-                a2_copy(d, k).wait_send()
-            a3_copy(d, k).wait_send()
-        for q in range(2):
-            if d:
-                remote(NFS.at[q], NF.at[q, cross], ns.at[q, d], nr.at[q, d], slab, cr(d)).wait_send()
-                e2_copy(q, d).wait_send()
-            e1_copy(q, d).wait_send()
-    for pair in pairs + v_edges + [pr_x, pr_y, p1_x, p1_y, p2_x, p2_y]:
-        for copy in pair:
-            copy.wait_send()
+    for copy in p2_x + p2_y:
+        copy.wait_send()
     f1_sends(lambda copy: copy.wait_send())
     for copy in outs:
         copy.wait()

time: 73.5 us -> 73 us (level); the launches traced: 72.4 us -> 72.8 us
  no operation moved by 1% of the time
where the time goes in v5:
time: 73 us; the launch traced here: 72.8 us
  Pallas kernels  72.2 us (99%)
    pallas_call x1, Pallas kernels, body(): pl.pallas_call(kernel, out_shape=(jax.ShapeDtypeStruct(velocity.shape, F3...  69.2 us
    pallas_call x1, Pallas kernels, body(): pl.pallas_call(finish_kernel, out_shape=(jax.ShapeDtypeStruct(velocity.sh...  2.98 us

profile of v5, /device:TPU:6, one launch (start us, length us, event | category | flops | bytes accessed | tf_op | source)
XLA Modules:
  0.0 72.8 jit_solution(15888799601401654434)
XLA Ops:
  0.6 69.2 %shard_map.95 = (f32[3,16,32,256]{3,2,1,0:T(8,128)}, f32[16,32,256]{2,1,0:T(8,128)}, f32[3,2,40,256]{3,2,1,0:T(8,128)}) custom-call(f32[3,16,32,256]{3,2,1,0:T(8,128)} %vel.1, f32[16,32,256]{2,1,0:T(8,128)} %pres.1, bf16[8,2,128,1024]{3,2,1,0:T(8,128)(2,1)} %bitcast.6, f32[8,3,128]{2,1,0:T(4,128)} %bitcast.9, s32[1024,256]{1,0:T(8,128)} %cells.1, ...), custom_call_target="tpu_custom_call" | custom-call | tf_op jit(solution)/shard_map/pallas_call | solution.py:660
  69.9 3.0 %shard_map.96 = (f32[3,16,32,256]{3,2,1,0:T(8,128)}, f32[16,32,256]{2,1,0:T(8,128)}) custom-call(f32[3,16,32,256]{3,2,1,0:T(8,128)} %get-tuple-element.5.ov, f32[16,32,256]{2,1,0:T(8,128)} %get-tuple-element.6.p2, f32[3,2,40,256]{3,2,1,0:T(8,128)} %get-tuple-element.7.push_in), custom_call_target="tpu_custom_call" | custom-call | tf_op jit(solution)/shard_map/pallas_call | solution.py:694
